TPU v7x, 32 devices: a whole 2x2x4 slice. The times are simulated.
32 devices in a mesh: tensor: 4 (over y, core), dp: 8 (over z, x).
Axes of the slice: x: 2, y: 2, z: 4, core: 2. Of those that a mesh axis runs over, the one named last changes fastest.
Arguments:
- inputs: bfloat16 [4096, 512], P('dp'), may hold values from -6 to 6
- norm_gains: bfloat16 [5, 512], replicated, may hold values from 0.25 to 1.75
- early_up: bfloat16 [512, 2048], P(None, 'tensor'), may hold values from -0.25 to 0.25
- early_down: bfloat16 [2048, 512], P('tensor'), may hold values from -0.25 to 0.25
- query_key_value: bfloat16 [512, 3, 512], P(None, None, 'tensor'), may hold values from -0.25 to 0.25
- position_weight: bfloat16 [512, 512], P(None, 'tensor'), may hold values from -0.25 to 0.25
- position_bias: bfloat16 [2, 8, 64], P(None, 'tensor'), may hold values from -3 to 3
- attention_out: bfloat16 [512, 512], P('tensor'), may hold values from -0.75 to 0.75
- pointwise_in: bfloat16 [512, 2, 512], P(None, None, 'tensor'), may hold values from -0.25 to 0.25
- depthwise: bfloat16 [31, 512], P(None, 'tensor'), may hold values from -1 to 1
- batch_gain: bfloat16 [512], P('tensor'), may hold values from 0.25 to 1.75
- batch_bias: bfloat16 [512], P('tensor'), may hold values from -3 to 3
- pointwise_out: bfloat16 [512, 512], P('tensor'), may hold values from -0.375 to 0.375
- late_up: bfloat16 [512, 2048], P(None, 'tensor'), may hold values from -0.25 to 0.25
- late_down: bfloat16 [2048, 512], P('tensor'), may hold values from -0.25 to 0.25
- output_cotangent: bfloat16 [4096, 512], P('dp'), may hold values from -6 to 6
Outputs:
- layer_output: bfloat16 [4096, 512], P('dp')
- input_gradient: float32 [4096, 512], P('dp')
- gains_gradient: float32 [5, 512], replicated
- early_up_gradient: float32 [512, 2048], P(None, 'tensor')
- early_down_gradient: float32 [2048, 512], P('tensor')
- query_key_value_gradient: float32 [512, 3, 512], P(None, None, 'tensor')
- position_weight_gradient: float32 [512, 512], P(None, 'tensor')
- position_bias_gradient: float32 [2, 8, 64], P(None, 'tensor')
- attention_out_gradient: float32 [512, 512], P('tensor')
- pointwise_in_gradient: float32 [512, 2, 512], P(None, None, 'tensor')
- depthwise_gradient: float32 [31, 512], P(None, 'tensor')
- batch_gain_gradient: float32 [512], P('tensor')
- batch_bias_gradient: float32 [512], P('tensor')
- pointwise_out_gradient: float32 [512, 512], P('tensor')
- late_up_gradient: float32 [512, 2048], P(None, 'tensor')
- late_down_gradient: float32 [2048, 512], P('tensor')
All inputs are finite; a program needn't handle non-finite values.
Results may differ from a plain program's by a relative error of at most 0.02.
Values sent between devices are 32-bit elements; how exact they have to be, the bound alone decides.
A program may use at most 128 MiB of HBM per device.

v0:
```python
import math

import jax
import jax.numpy as jnp
from jax import lax
from jax.sharding import PartitionSpec as P

LENGTH = 512


EPS = 1e-05


def plain_round(v):
    return lax.optimization_barrier(v.astype(jnp.bfloat16)).astype(jnp.float32)


def plain_same(v):
    return v


def value_keep(v):
    return (plain_round(v), None)


def value_pass(kept, grad):
    return (grad,)


def grad_keep(v):
    return (v, None)


def grad_round(kept, grad):
    return (plain_round(grad),)


def low(v):
    rounder = jax.custom_vjp(plain_round)
    rounder.defvjp(value_keep, value_pass)
    return rounder(v)


def low_back(v):
    rounder = jax.custom_vjp(plain_same)
    rounder.defvjp(grad_keep, grad_round)
    return rounder(v)


def matmul(first_factor, second_factor):
    return jnp.dot(first_factor, second_factor, preferred_element_type=jnp.float32)


def layer_norm(values, gain_row):
    centre = values - jnp.mean(values, axis=-1, keepdims=True)
    spread = jnp.mean(centre * centre, axis=-1, keepdims=True)
    return centre * lax.rsqrt(spread + EPS) * gain_row


def sinusoid_table(length, model_width):
    offsets = (length - 1 - jnp.arange(2 * length - 1)).astype(jnp.float32)
    frequency = jnp.exp(
        jnp.arange(0, model_width, 2).astype(jnp.float32) * (-math.log(10000.0) / model_width)
    )
    phases = offsets[:, None] * frequency[None, :]
    return jnp.stack([jnp.sin(phases), jnp.cos(phases)], axis=-1).reshape(
        2 * length - 1, model_width
    )


def relative_shift(scores):
    head_count, length, span_size = scores.shape
    padded = jnp.pad(scores, ((0, 0), (0, 0), (1, 0)))
    padded = padded.reshape(head_count, 2 * length, length)[:, 1:]
    return padded.reshape(head_count, length, span_size)[:, :, :length]


def feed_forward(values, gain_row, weight_in, weight_out):
    normed = low(layer_norm(values, gain_row))
    hidden = low_back(matmul(normed, weight_in))
    active = low(jax.nn.silu(hidden))
    return low_back(matmul(active, weight_out))


def sequence_core(sequence, sinusoid, weight_pos, biases):
    length = sequence.shape[0]
    head_count = sequence.shape[2]
    head_size = sequence.shape[3]
    queries = sequence[:, 0]
    key_rows = low(sequence[:, 1])
    values = low(sequence[:, 2])
    position = low(low_back(matmul(sinusoid, weight_pos))).reshape(
        2 * length - 1, head_count, head_size
    )
    with_content = low(queries + biases[0])
    with_position = low(queries + biases[1])
    content = jnp.einsum("ihd,jhd->hij", with_content, key_rows, preferred_element_type=jnp.float32)
    relative = relative_shift(
        jnp.einsum("ihd,rhd->hir", with_position, position, preferred_element_type=jnp.float32)
    )
    scores = low_back((content + relative) * (1.0 / math.sqrt(head_size)))
    weights = low(jax.nn.softmax(scores, axis=-1))
    return jnp.einsum("hij,jhd->ihd", weights, values, preferred_element_type=jnp.float32)


def attention(values, gain_row, weight_qkv, weight_pos, biases, weight_out):
    model_width = weight_qkv.shape[0]
    local_width = weight_qkv.shape[2]
    head_count = biases.shape[1]
    head_size = biases.shape[2]
    normed = low(layer_norm(values, gain_row))
    mixed_rows = low_back(matmul(normed, weight_qkv.reshape(model_width, 3 * local_width)))
    mixed_rows = mixed_rows.reshape(-1, LENGTH, 3, head_count, head_size)
    sinusoid = low(sinusoid_table(LENGTH, model_width))
    per_sequence = jax.checkpoint(
        lambda sequence: sequence_core(sequence, sinusoid, weight_pos, biases)
    )
    attended = lax.map(per_sequence, mixed_rows).reshape(-1, local_width)
    attended = low(low_back(attended))
    return low_back(matmul(attended, weight_out))


def depthwise_conv(gated, kernel):
    half = kernel.shape[0] // 2
    return lax.conv_general_dilated(
        gated,
        kernel[:, None, :],
        (1,),
        [(half, half)],
        dimension_numbers=("NWC", "WIO", "NWC"),
        feature_group_count=gated.shape[2],
        precision=lax.Precision.HIGHEST,
    )


def conv_front(values, gain_row, weight_in, kernel):
    channels = kernel.shape[1]
    normed = low(layer_norm(values, gain_row))
    paired = low_back(matmul(normed, weight_in.reshape(weight_in.shape[0], 2 * channels))).reshape(
        -1, 2, channels
    )
    gated = paired[:, 0] * jax.nn.sigmoid(paired[:, 1])
    return depthwise_conv(gated.reshape(-1, LENGTH, channels), kernel)


def conv_back(mixed_rows, batch_mean, batch_var, scale_row, shift_row, weight_out):
    scaled = (mixed_rows - batch_mean) * lax.rsqrt(batch_var + EPS) * scale_row + shift_row
    swished = low(jax.nn.silu(scaled)).reshape(-1, mixed_rows.shape[2])
    return low_back(matmul(swished, weight_out))


def add_branch(base_rows, partial_value, factor):
    return base_rows + factor * lax.psum(partial_value, "tensor")


def add_gradient(base_rows, cotangent_in, gain_piece):
    cotangent_sum, gain_total = lax.psum((cotangent_in, gain_piece), "tensor")
    return (base_rows + cotangent_sum, gain_total)


def per_device(
    inputs,
    norm_gains,
    early_up,
    early_down,
    query_key_value,
    position_weight,
    position_bias,
    attention_out,
    pointwise_in,
    depthwise,
    batch_gain,
    batch_bias,
    pointwise_out,
    late_up,
    late_down,
    output_cotangent,
):
    stream = inputs.astype(jnp.float32)
    gain_rows = norm_gains.astype(jnp.float32)
    early_in = early_up.astype(jnp.float32)
    early_back = early_down.astype(jnp.float32)
    project_qkv = query_key_value.astype(jnp.float32)
    project_pos = position_weight.astype(jnp.float32)
    query_bias = position_bias.astype(jnp.float32)
    project_out = attention_out.astype(jnp.float32)
    point_first = pointwise_in.astype(jnp.float32)
    depth_taps = depthwise.astype(jnp.float32)
    scale_row = batch_gain.astype(jnp.float32)
    shift_row = batch_bias.astype(jnp.float32)
    point_second = pointwise_out.astype(jnp.float32)
    late_in = late_up.astype(jnp.float32)
    late_back = late_down.astype(jnp.float32)
    first_part, first_pull = jax.vjp(feed_forward, stream, gain_rows[0], early_in, early_back)
    after_first = add_branch(stream, first_part, 0.5)
    second_part, second_pull = jax.vjp(
        attention, after_first, gain_rows[1], project_qkv, project_pos, query_bias, project_out
    )
    after_second = add_branch(after_first, second_part, 1.0)
    mixed_rows, front_pull = jax.vjp(
        conv_front, after_second, gain_rows[2], point_first, depth_taps
    )
    token_count = mixed_rows.shape[0] * mixed_rows.shape[1] * lax.axis_size("dp")
    sum_values, sum_squares = lax.psum(
        (jnp.sum(mixed_rows, axis=(0, 1)), jnp.sum(mixed_rows * mixed_rows, axis=(0, 1))), "dp"
    )
    batch_mean = sum_values / token_count
    batch_var = sum_squares / token_count - batch_mean * batch_mean
    third_part, back_pull = jax.vjp(
        conv_back, mixed_rows, batch_mean, batch_var, scale_row, shift_row, point_second
    )
    after_third = add_branch(after_second, third_part, 1.0)
    fourth_part, fourth_pull = jax.vjp(feed_forward, after_third, gain_rows[3], late_in, late_back)
    after_fourth = add_branch(after_third, fourth_part, 0.5)
    result, final_pull = jax.vjp(layer_norm, after_fourth, gain_rows[4])
    grad_four, final_gain = final_pull(output_cotangent.astype(jnp.float32))
    cotangent_in, gain_piece, late_in_grad, late_back_grad = fourth_pull(0.5 * grad_four)
    grad_three, gain_four = add_gradient(grad_four, cotangent_in, gain_piece)
    final_gain, gain_four, late_in_grad, late_back_grad = (
        final_gain,
        gain_four,
        late_in_grad,
        late_back_grad,
    )
    direct_grad, mean_grad, var_grad, scale_grad, shift_grad, second_point_grad = back_pull(
        grad_three
    )
    mean_grad, var_grad = lax.psum((mean_grad, var_grad), "dp")
    mixed_grad = (
        direct_grad + (mean_grad + 2.0 * var_grad * (mixed_rows - batch_mean)) / token_count
    )
    cotangent_in, gain_piece, first_point_grad, depth_grad = front_pull(mixed_grad)
    grad_two, gain_two = add_gradient(grad_three, cotangent_in, gain_piece)
    gain_two, scale_grad, shift_grad, second_point_grad, first_point_grad, depth_grad = (
        gain_two,
        scale_grad,
        shift_grad,
        second_point_grad,
        first_point_grad,
        depth_grad,
    )
    cotangent_in, gain_piece, qkv_grad, pos_grad, bias_grad, out_grad = second_pull(grad_two)
    grad_one, gain_one = add_gradient(grad_two, cotangent_in, gain_piece)
    gain_one, qkv_grad, pos_grad, bias_grad, out_grad = (
        gain_one,
        qkv_grad,
        pos_grad,
        bias_grad,
        out_grad,
    )
    cotangent_in, gain_piece, early_in_grad, early_back_grad = first_pull(0.5 * grad_one)
    grad_zero, gain_zero = add_gradient(grad_one, cotangent_in, gain_piece)
    gain_zero, early_in_grad, early_back_grad = (gain_zero, early_in_grad, early_back_grad)
    gain_grads = jnp.stack([gain_zero, gain_one, gain_two, gain_four, final_gain])
    (
        gain_grads,
        early_in_grad,
        early_back_grad,
        qkv_grad,
        pos_grad,
        bias_grad,
        out_grad,
        first_point_grad,
        depth_grad,
        scale_grad,
        shift_grad,
        second_point_grad,
        late_in_grad,
        late_back_grad,
    ) = lax.psum(
        (
            gain_grads,
            early_in_grad,
            early_back_grad,
            qkv_grad,
            pos_grad,
            bias_grad,
            out_grad,
            first_point_grad,
            depth_grad,
            scale_grad,
            shift_grad,
            second_point_grad,
            late_in_grad,
            late_back_grad,
        ),
        "dp",
    )
    return (
        result.astype(jnp.bfloat16),
        grad_zero,
        gain_grads,
        early_in_grad,
        early_back_grad,
        qkv_grad,
        pos_grad,
        bias_grad,
        out_grad,
        first_point_grad,
        depth_grad,
        scale_grad,
        shift_grad,
        second_point_grad,
        late_in_grad,
        late_back_grad,
    )


def solution(mesh):
    return jax.shard_map(
        per_device,
        mesh=mesh,
        in_specs=(
            P("dp", None),
            P(),
            P(None, "tensor"),
            P("tensor", None),
            P(None, None, "tensor"),
            P(None, "tensor"),
            P(None, "tensor", None),
            P("tensor", None),
            P(None, None, "tensor"),
            P(None, "tensor"),
            P("tensor"),
            P("tensor"),
            P("tensor", None),
            P(None, "tensor"),
            P("tensor", None),
            P("dp", None),
        ),
        out_specs=(
            P("dp", None),
            P("dp", None),
            P(),
            P(None, "tensor"),
            P("tensor", None),
            P(None, None, "tensor"),
            P(None, "tensor"),
            P(None, "tensor", None),
            P("tensor", None),
            P(None, None, "tensor"),
            P(None, "tensor"),
            P("tensor"),
            P("tensor"),
            P("tensor", None),
            P(None, "tensor"),
            P("tensor", None),
        ),
        check_vma=False,
    )
```

profile of v0, /device:TPU:0, one launch (start us, length us, event | category | flops | bytes accessed | tf_op | source)
XLA Modules:
  0.0 733.0 jit_solution(10238060074771365690)
XLA Ops:
  17.1 31.0 %fusion.20 = (bf16[1023,256,1]{0,2,1:T(2,128)(2,1)S(1)}, bf16[1023,256,1]{0,2,1:T(2,128)(2,1)S(1)}) fusion(f32[1023]{0:T(1024)S(1)} %subtract_convert_fusion, f32[256]{0:T(256)S(1)} %multiply_exponential_fusion), kind=kLoop, calls=%fused_computation.49 | loop fusion | flops 785664 | bytes 1052668 | tf_op jit(solution)/shard_map/convert.3
  48.1 2.5 pad_maximum_fusion
  59.9 3.2 pad.50
  63.1 5.0 reshape.456
  68.1 4.9 slice.118
  73.0 6.5 reshape.457
  79.5 3.1 slice.119
  82.6 2.9 copy.109
  85.5 3.8 fusion.102
  94.2 37.0 %all-reduce.28.cloned.1.call-done = f32[512,512]{1,0:T(8,128)} async-done(((f32[512,512]{1,0:T(8,128)}), f32[512,512]{1,0:T(8,128)}) %all-reduce.28.cloned.1.call-update) | async-done | bytes 1048592 | tf_op jit(solution)/shard_map/psum | solution.py:153
  134.6 21.5 %all-reduce.13 = (f32[128]{0:T(128)S(1)}, f32[128]{0:T(128)S(1)}) all-reduce(f32[128]{0:T(128)S(1)} %get-tuple-element.85, f32[128]{0:T(128)S(1)} %get-tuple-element.84), channel_id=1, replica_groups=mesh['tensor'=4,'dp'=8] {'dp'}, use_global_device_ids=true, to_apply=%region_11.12 | all-reduce | flops 256 | bytes 2048 | tf_op jit(solution)/shard_map/psum | solution.py:204
  159.8 32.9 %all-reduce.30.cloned.1.call-done = f32[512,512]{1,0:T(8,128)} async-done(((f32[512,512]{1,0:T(8,128)}), f32[512,512]{1,0:T(8,128)}) %all-reduce.30.cloned.1.call-update) | async-done | bytes 1048592 | tf_op jit(solution)/shard_map/psum | solution.py:153
  199.7 36.5 %all-reduce.32.cloned.1.call-done = f32[512,512]{1,0:T(8,128)} async-done(((f32[512,512]{1,0:T(8,128)}), f32[512,512]{1,0:T(8,128)}) %all-reduce.32.cloned.1.call-update) | async-done | bytes 1048592 | tf_op jit(solution)/shard_map/psum | solution.py:153
  253.0 2.5 fusion.117
  255.5 25.7 %all-reduce.34.cloned.1.call-done = f32[512,512]{1,0:T(8,128)} async-done(((f32[512,512]{1,0:T(8,128)}), f32[512,512]{1,0:T(8,128)}) %all-reduce.34.cloned.1.call-update) | async-done | bytes 1048592 | tf_op jit(solution)/shard_map/psum | solution.py:157
  285.5 22.0 %all-reduce.12 = (f32[128]{0:T(128)}, f32[128]{0:T(128)}) all-reduce(f32[128]{0:T(128)} %neg.55, f32[128]{0:T(128)} %multiply_multiply_fusion.5), channel_id=1, replica_groups=mesh['tensor'=4,'dp'=8] {'dp'}, use_global_device_ids=true, to_apply=%region_26.27 | all-reduce | flops 256 | bytes 2048 | tf_op jit(solution)/shard_map/psum | solution.py:228
  320.7 2.7 fusion.116
  327.5 25.9 %all-reduce.36.cloned.1.call-done = f32[512,512]{1,0:T(8,128)} async-done(((f32[512,512]{1,0:T(8,128)}), f32[512,512]{1,0:T(8,128)}) %all-reduce.36.cloned.1.call-update) | async-done | bytes 1048592 | tf_op jit(solution)/shard_map/psum | solution.py:157
  353.4 2.7 fusion.89
  362.4 3.2 pad.53
  365.6 5.0 reshape.463
  370.5 4.9 slice.135
  375.4 6.5 reshape.464
  385.4 2.7 fusion.103
  396.1 6.1 reshape.465
  404.1 2.9 reshape.466
  419.0 30.1 %all-reduce.38.cloned.1.call-done = f32[512,512]{1,0:T(8,128)} async-done(((f32[512,512]{1,0:T(8,128)}), f32[512,512]{1,0:T(8,128)}) %all-reduce.38.cloned.1.call-update) | async-done | bytes 1048592 | tf_op jit(solution)/shard_map/psum | solution.py:157
  458.8 5.9 fusion.106
  464.7 6.3 all-reduce.15
  471.1 38.5 %all-reduce.11 = (f32[5,512]{1,0:T(8,128)}, f32[2,2,64]{2,1,0:T(2,128)}, f32[31,128]{1,0:T(8,128)}, f32[128]{0:T(128)}, f32[128]{0:T(128)}) all-reduce(f32[5,512]{1,0:T(8,128)S(1)} %stack.27, f32[2,2,64]{2,1,0:T(2,128)S(1)} %pad_add_fusion, f32[31,128]{1,0:T(8,128)S(1)} %bitcast.232, ...), channel_id=1, replica_groups=mesh['tensor'=4,'dp'=8] {'dp'}, use_global_device_ids=true, to_apply=%region_50.51 | all-reduce | flops 7040 | bytes 56320 | tf_op jit(solution)/shard_map/psum | solution.py:270
  509.6 2.4 add.310
  512.0 204.9 %all-reduce.42.cloned.1.call-done = (f32[512,512]{1,0:T(8,128)}, f32[512,512]{1,0:T(8,128)}, f32[512,3,128]{2,0,1:T(8,128)}, f32[512,128]{1,0:T(8,128)}, f32[128...) async-done(((f32[512,512]{1,0:T(8,128)}, f32[512,512]{1,0:T(8,128)}, f32[512,3,128]{2,0,1:T(8,128)}, ...) | async-done | bytes 6291472 | tf_op jit(solution)/shard_map/psum | solution.py:270
  (457 shorter events, 125.5 us)
Async XLA Ops:
  7.2 188.7 %copy-start = (bf16[512,512]{1,0:T(8,128)(2,1)S(1)}, bf16[512,512]{1,0:T(8,128)(2,1)}, u32[]{:S(2)}) copy-start(bf16[512,512]{1,0:T(8,128)(2,1)} %param.29) | copy-start | bytes 1572868
  7.2 6.1 copy-start.70
  7.2 48.8 %all-reduce.26.cloned.1.call-start = ((), (), s32[]{:S(2)}) async-start(), calls=%async_computation | async-start | bytes 2097152 | tf_op jit(solution)/shard_map/psum | solution.py:153
  8.6 6.2 copy-start.79
  12.0 45.8 %copy-start.110 = (f32[1,512]{1,0:T(1,128)}, f32[1,512]{1,0:T(1,128)S(1)}, u32[]{:S(2)}) copy-start(f32[1,512]{1,0:T(1,128)S(1)} %get-tuple-element.159) | copy-start | bytes 6148
  12.0 120.9 %copy-start.93 = (f32[1,512]{1,0:T(1,128)}, f32[1,512]{1,0:T(1,128)S(1)}, u32[]{:S(2)}) copy-start(f32[1,512]{1,0:T(1,128)S(1)} %get-tuple-element.158) | copy-start | bytes 6148
  17.0 114.1 %all-reduce.28.cloned.1.call-start = ((), (), s32[]{:S(2)}) async-start(), calls=%async_computation.1 | async-start | bytes 2097152 | tf_op jit(solution)/shard_map/psum | solution.py:153
  50.8 7.5 %copy-start.38 = (bf16[512,3,128]{0,2,1:T(8,128)(2,1)}, bf16[512,3,128]{0,2,1:T(8,128)(2,1)S(1)}, u32[]{:S(2)}) copy-start(bf16[512,3,128]{0,2,1:T(8,128)(2,1)S(1)} %copy.60) | copy-start | bytes 1179652
  51.7 5.8 copy-start.5
  57.4 73.7 %copy-start.2 = (f32[512,512]{1,0:T(8,128)}, f32[512,512]{1,0:T(8,128)S(1)}, u32[]{:S(2)}) copy-start(f32[512,512]{1,0:T(8,128)S(1)} %get-tuple-element.137) | copy-start | bytes 3145732
  93.5 99.2 %all-reduce.30.cloned.1.call-start = ((), (), s32[]{:S(2)}) async-start(), calls=%async_computation.2 | async-start | bytes 2097152 | tf_op jit(solution)/shard_map/psum | solution.py:153
  94.0 62.7 %copy-start.120 = (f32[128]{0:T(128)}, f32[128]{0:T(128)S(1)}, u32[]{:S(2)}) copy-start(f32[128]{0:T(128)S(1)} %convert_element_type.256) | copy-start | bytes 1540
  134.6 23.8 %copy-start.57 = (bf16[128,512]{1,0:T(8,128)(2,1)S(1)}, bf16[128,512]{1,0:T(8,128)(2,1)}, u32[]{:S(2)}) copy-start(bf16[128,512]{1,0:T(8,128)(2,1)} %param.28) | copy-start | bytes 393220
  159.8 76.5 %all-reduce.32.cloned.1.call-start = ((), (), s32[]{:S(2)}) async-start(), calls=%async_computation.3 | async-start | bytes 2097152 | tf_op jit(solution)/shard_map/psum | solution.py:153
  199.6 81.6 %all-reduce.34.cloned.1.call-start = ((), (), s32[]{:S(2)}) async-start(), calls=%async_computation.4 | async-start | bytes 2097152 | tf_op jit(solution)/shard_map/psum | solution.py:157
  244.6 108.8 %all-reduce.36.cloned.1.call-start = ((), (), s32[]{:S(2)}) async-start(), calls=%async_computation.5 | async-start | bytes 2097152 | tf_op jit(solution)/shard_map/psum | solution.py:157
  245.5 7.5 %copy-start.31 = (bf16[512,512]{1,0:T(8,128)(2,1)S(1)}, bf16[512,512]{1,0:T(8,128)(2,1)}, u32[]{:S(2)}) copy-start(bf16[512,512]{1,0:T(8,128)(2,1)} %copy-done.30) | copy-start | bytes 1572868
  247.0 34.2 %copy-start.9 = (f32[512,512]{1,0:T(8,128)S(1)}, f32[512,512]{1,0:T(8,128)}, u32[]{:S(2)}) copy-start(f32[512,512]{1,0:T(8,128)} %copy-done.8) | copy-start | bytes 3145732
  282.9 28.8 %copy-start.15 = (bf16[512,512]{1,0:T(8,128)(2,1)}, bf16[512,512]{1,0:T(8,128)(2,1)S(1)}, u32[]{:S(2)}) copy-start(bf16[512,512]{1,0:T(8,128)(2,1)S(1)} %fusion.67) | copy-start | bytes 1572868
  320.4 6.1 copy-start.16
  320.4 128.6 %all-reduce.38.cloned.1.call-start = ((), (), s32[]{:S(2)}) async-start(), calls=%async_computation.6 | async-start | bytes 2097152 | tf_op jit(solution)/shard_map/psum | solution.py:157
  323.4 30.1 %copy-start.92 = (f32[512]{0:T(512)S(1)}, f32[512]{0:T(512)}, u32[]{:S(2)}) copy-start(f32[512]{0:T(512)} %copy-done.91) | copy-start | bytes 6148
  327.5 29.4 %copy-start.61 = (bf16[128,512]{1,0:T(8,128)(2,1)S(1)}, bf16[128,512]{1,0:T(8,128)(2,1)}, u32[]{:S(2)}) copy-start(bf16[128,512]{1,0:T(8,128)(2,1)} %param.23) | copy-start | bytes 393220
  327.5 29.9 %copy-start.109 = (f32[2,2,64]{2,1,0:T(2,128)S(1)}, f32[2,2,64]{2,1,0:T(2,128)}, u32[]{:S(2)}) copy-start(f32[2,2,64]{2,1,0:T(2,128)} %copy-done.108) | copy-start | bytes 3076
  412.4 97.2 %all-reduce.40.cloned.1.call-start = ((), (), s32[]{:S(2)}) async-start(), calls=%async_computation.7 | async-start | bytes 2097152 | tf_op jit(solution)/shard_map/psum | solution.py:157
  417.9 31.2 %copy-start.21 = (f32[512,512]{1,0:T(8,128)S(1)}, f32[512,512]{1,0:T(8,128)}, u32[]{:S(2)}) copy-start(f32[512,512]{1,0:T(8,128)} %get-tuple-element.117) | copy-start | bytes 3145732
  454.6 262.3 %all-reduce.42.cloned.1.call-start = ((), (), s32[]{:S(2)}) async-start(), calls=%async_computation.8 | async-start | bytes 12582912 | tf_op jit(solution)/shard_map/psum | solution.py:270
  458.8 5.9 copy-start.118
  458.8 5.9 copy-start.119
  458.8 12.3 %copy-start.117 = (f32[512]{0:T(512)S(1)}, f32[512]{0:T(512)}, u32[]{:S(2)}) copy-start(f32[512]{0:T(512)} %get-tuple-element.82) | copy-start | bytes 6148
  458.8 12.3 %copy-start.123 = (f32[128]{0:T(128)S(1)}, f32[128]{0:T(128)}, u32[]{:S(2)}) copy-start(f32[128]{0:T(128)} %get-tuple-element.88) | copy-start | bytes 1540
  458.8 12.3 %copy-start.124 = (f32[128]{0:T(128)S(1)}, f32[128]{0:T(128)}, u32[]{:S(2)}) copy-start(f32[128]{0:T(128)} %get-tuple-element.89) | copy-start | bytes 1540
  (114 other events, 217.0 us)
Sparse Core Ops, SparseCore 0:
  17.1 38.8 all-reduce.25
  93.7 37.4 all-reduce.27
  159.9 32.8 all-reduce.29
  199.7 36.4 all-reduce.31
  244.7 36.4 all-reduce.33
  320.6 32.8 all-reduce.35
  412.5 36.5 all-reduce.37
  454.7 36.6 all-reduce.39
  498.2 218.6 all-reduce.41
where the time goes:
time: 744 us; the launch traced here: 733 us
  waiting for transfers between devices  395 us (53%)
  local copies, waits for them, and re-layouts  102 us (14%)
  blocking collectives  88.3 us (12%)
  other arithmetic  75.2 us (10%)
  matrix products  56 us (8%)
  between operations  16 us (2%)
    psum x1, waiting for transfers between devices, per_device(): lax.psum((gain_grads, early_in_grad, early_back_grad, qkv_grad, pos_grad,...  205 us
    psum x4, waiting for transfers between devices, add_branch(): return base_rows + factor * lax.psum(partial_value, 'tensor')  108 us
    psum x4, waiting for transfers between devices, add_gradient(): cotangent_sum, gain_total = lax.psum((cotangent_in, gain_piece), 'tensor')  81.7 us
    psum x1, blocking collectives, per_device(): lax.psum((gain_grads, early_in_grad, early_back_grad, qkv_grad, pos_grad,...  38.5 us
    dot_general x27, matrix products, matmul(): jnp.dot(first_factor, second_factor, preferred_element_type=jnp.float32)  33.1 us
    another operation x2, other arithmetic  32.2 us
    unnamed x287, local copies, waits for them, and re-layouts  23.3 us
    psum x1, blocking collectives, per_device(): mean_grad, var_grad = lax.psum((mean_grad, var_grad), 'dp')  22 us
  transfers between devices with their start and end apart: 9, of which 8 were waited for; matrix products, arithmetic and copies ran while one was open for 10% of the time, Pallas kernels for 0%

commit v1 on v0

v1 whole, which is shorter than its diff:
```python
import functools
import math

import jax
import jax.numpy as jnp
import ml_dtypes
import numpy as np
from jax import lax
from jax.experimental import pallas as pl
from jax.experimental.pallas import tpu as pltpu
from jax.sharding import PartitionSpec as P

LENGTH = 512


EPS = 1e-05


def plain_round(v):
    return lax.optimization_barrier(v.astype(jnp.bfloat16)).astype(jnp.float32)


def plain_same(v):
    return v


def value_keep(v):
    return (plain_round(v), None)


def value_pass(kept, grad):
    return (grad,)


def grad_keep(v):
    return (v, None)


def grad_round(kept, grad):
    return (plain_round(grad),)


def low(v):
    rounder = jax.custom_vjp(plain_round)
    rounder.defvjp(value_keep, value_pass)
    return rounder(v)


def low_back(v):
    rounder = jax.custom_vjp(plain_same)
    rounder.defvjp(grad_keep, grad_round)
    return rounder(v)


def matmul(first_factor, second_factor):
    return jnp.dot(first_factor, second_factor, preferred_element_type=jnp.float32)


def layer_norm(values, gain_row):
    centre = values - jnp.mean(values, axis=-1, keepdims=True)
    spread = jnp.mean(centre * centre, axis=-1, keepdims=True)
    return centre * lax.rsqrt(spread + EPS) * gain_row


MESH = pl.DeviceIdType.MESH
VMEM = pl.BlockSpec(memory_space=pltpu.VMEM)


def sinusoid_tables(length, model_width):
    offsets = (length - 1 - np.arange(2 * length - 1)).astype(np.float32)
    frequency = np.exp(
        np.arange(0, model_width, 2).astype(np.float32)
        * np.float32(-math.log(10000.0) / model_width)
    ).astype(np.float32)
    phases = offsets[:, None] * frequency[None, :]
    table = np.stack([np.sin(phases), np.cos(phases)], axis=-1).reshape(2 * length - 1, model_width)
    zero = np.zeros((1, model_width), np.float32)
    return (
        np.concatenate([table, zero]).astype(ml_dtypes.bfloat16),
        np.concatenate([table[::-1], zero]).astype(ml_dtypes.bfloat16),
    )


def tensor_kernel(factor, chunks, part, base, out, from_core, chip, from_row, send, recv):
    me = lax.axis_index("tensor")
    core = lax.rem(me, 2)
    sibling = me + 1 - 2 * core
    opposite = lax.rem(me + 2, 4)
    half = part.shape[0] // 2
    rows = half // chunks
    mine = core * half
    theirs = half - mine
    barrier = pltpu.get_barrier_semaphore()
    for other in (sibling, opposite):
        pl.semaphore_signal(barrier, inc=1, device_id={"tensor": other}, device_id_type=MESH)
    pl.semaphore_wait(barrier, 2)

    def span(start, c):
        return pl.ds(pl.multiple_of(start + c * rows, 8), rows)

    def remote(source, target, stage, c, device):
        return pltpu.make_async_remote_copy(
            src_ref=source,
            dst_ref=target,
            send_sem=send.at[stage, c],
            recv_sem=recv.at[stage, c],
            device_id={"tensor": device},
            device_id_type=MESH,
        )

    def first(c):
        return remote(part.at[span(theirs, c)], from_core.at[span(0, c)], 0, c, sibling)

    def second(c):
        return remote(chip.at[span(0, c)], from_row.at[span(0, c)], 1, c, opposite)

    def third(c):
        return remote(out.at[span(mine, c)], out.at[span(mine, c)], 2, c, sibling)

    for c in range(chunks):
        first(c).start()
    for c in range(chunks):
        first(c).wait_recv()
        chip[span(0, c), :] = part[span(mine, c), :] + from_core[span(0, c), :]
        second(c).start()
    for c in range(chunks):
        second(c).wait_recv()
        total = chip[span(0, c), :] + from_row[span(0, c), :]
        out[span(mine, c), :] = base[span(mine, c), :] + factor * total
        third(c).start()
    for c in range(chunks):
        first(c).wait_send()
        second(c).wait_send()
        third(c).wait_send()
        third(c).wait_recv()


def tensor_sum(base, part, factor, ident, chunks=8):
    rows, width = part.shape
    half = pltpu.VMEM((rows // 2, width), jnp.float32)
    return pl.pallas_call(
        functools.partial(tensor_kernel, factor, chunks),
        out_shape=jax.ShapeDtypeStruct((rows, width), jnp.float32),
        in_specs=[VMEM, VMEM],
        out_specs=VMEM,
        scratch_shapes=[
            half,
            half,
            half,
            pltpu.SemaphoreType.DMA((3, chunks)),
            pltpu.SemaphoreType.DMA((3, chunks)),
        ],
        compiler_params=pltpu.CompilerParams(
            collective_id=ident, has_side_effects=True, vmem_limit_bytes=16 * 2**20
        ),
        name="tensor_sum",
    )(part, base)


def exchange_kernel(axis, count, part, out, slots, send, recv):
    me = lax.axis_index(axis)
    barrier = pltpu.get_barrier_semaphore()

    def greet(step, carry):
        other = lax.rem(me + step, count)
        pl.semaphore_signal(barrier, inc=1, device_id={axis: other}, device_id_type=MESH)
        return carry

    lax.fori_loop(1, count, greet, 0)
    slots[me] = part[...]
    pl.semaphore_wait(barrier, count - 1)

    def copy(step):
        other = lax.rem(me + step, count)
        return pltpu.make_async_remote_copy(
            src_ref=part,
            dst_ref=slots.at[me],
            send_sem=send.at[step],
            recv_sem=recv.at[step],
            device_id={axis: other},
            device_id_type=MESH,
        )

    def begin(step, carry):
        copy(step).start()
        return carry

    def finish(step, carry):
        copy(step).wait_send()
        copy(step).wait_recv()
        return carry

    lax.fori_loop(1, count, begin, 0)
    lax.fori_loop(1, count, finish, 0)
    total = slots[0]
    for place in range(1, count):
        total = total + slots[place]
    out[...] = total


def exchange_sum(part, axis, ident):
    count = lax.axis_size(axis)
    return pl.pallas_call(
        functools.partial(exchange_kernel, axis, count),
        out_shape=jax.ShapeDtypeStruct(part.shape, jnp.float32),
        in_specs=[VMEM],
        out_specs=VMEM,
        scratch_shapes=[
            pltpu.VMEM((count,) + part.shape, jnp.float32),
            pltpu.SemaphoreType.DMA((count,)),
            pltpu.SemaphoreType.DMA((count,)),
        ],
        compiler_params=pltpu.CompilerParams(
            collective_id=ident, has_side_effects=True, vmem_limit_bytes=16 * 2**20
        ),
        name="exchange_" + axis,
    )(part)


def stack_rows(pieces, width):
    blocks = []
    starts = []
    filled = 0
    for piece in pieces:
        block = piece.reshape(-1, width)
        starts.append(filled)
        filled += block.shape[0]
        blocks.append(block)
    spare = -filled % 8
    if spare:
        blocks.append(jnp.zeros((spare, width), jnp.float32))
    return jnp.concatenate(blocks), starts


def exchange_many(pieces, axis, ident, width=128):
    packed, starts = stack_rows(pieces, width)
    summed = exchange_sum(packed, axis, ident)
    return [
        summed[start : start + piece.size // width].reshape(piece.shape)
        for piece, start in zip(pieces, starts)
    ]


def product(first_factor, second_factor, first_axis, second_axis):
    return lax.dot_general(
        first_factor,
        second_factor,
        (((first_axis,), (second_axis,)), ((), ())),
        preferred_element_type=jnp.float32,
    )


def head_mask(shape, head, head_size):
    lane = lax.broadcasted_iota(jnp.int32, shape, 1)
    return (lane >= head * head_size) & (lane < (head + 1) * head_size)


def attend_kernel(head_count, mixed, position, biases, out, weights, with_content, with_position):
    length = mixed.shape[0]
    width = out.shape[1]
    head_size = width // head_count
    queries = mixed[:, :width]
    keys = mixed[:, width : 2 * width].astype(jnp.bfloat16)
    values = mixed[:, 2 * width :].astype(jnp.bfloat16)
    with_content[...] = (queries + biases[0:1, :]).astype(jnp.bfloat16)
    with_position[...] = (queries + biases[1:2, :]).astype(jnp.bfloat16)
    attended = jnp.zeros((length, width), jnp.float32)
    for head in range(head_count):
        mask = head_mask((length, width), head, head_size)
        zero = jnp.zeros((length, width), jnp.bfloat16)
        content = product(jnp.where(mask, with_content[...], zero), keys, 1, 1)
        spread = product(jnp.where(mask, with_position[...], zero), position[...], 1, 1)
        relative = pltpu.roll(spread, length + 1, 1, stride=1, stride_axis=0)[:, :length]
        scores = (content + relative) * (1.0 / math.sqrt(head_size))
        top = jnp.max(scores, axis=1, keepdims=True)
        powers = jnp.exp(scores - top)
        share = (powers / jnp.sum(powers, axis=1, keepdims=True)).astype(jnp.bfloat16)
        weights[head] = share
        attended = jnp.where(mask, product(share, values, 1, 0), attended)
    out[...] = attended.astype(jnp.bfloat16)


def attend(mixed, position, biases, head_count):
    length = mixed.shape[0]
    width = mixed.shape[1] // 3
    flat = jax.ShapeDtypeStruct((length, width), jnp.bfloat16)
    return pl.pallas_call(
        functools.partial(attend_kernel, head_count),
        out_shape=(
            flat,
            jax.ShapeDtypeStruct((head_count, length, length), jnp.bfloat16),
            flat,
            flat,
        ),
        in_specs=[VMEM] * 3,
        out_specs=(VMEM,) * 4,
        compiler_params=pltpu.CompilerParams(vmem_limit_bytes=32 * 2**20),
        name="attend",
    )(mixed, position, biases)


def attend_back_kernel(
    head_count,
    grad_ref,
    mixed,
    reversed_position,
    weights,
    with_content,
    with_position,
    mixed_grad,
    position_grad,
    bias_grad,
):
    length, width = grad_ref.shape
    head_size = width // head_count
    row = lax.broadcasted_iota(jnp.int32, (length, length), 0)
    column = lax.broadcasted_iota(jnp.int32, (length, length), 1)
    flip = (row + column == length - 1).astype(jnp.float32).astype(jnp.bfloat16)
    zero = jnp.zeros((length, width), jnp.bfloat16)
    grad = grad_ref[...]
    keys = product(flip, mixed[:, width : 2 * width].astype(jnp.bfloat16), 1, 0).astype(jnp.bfloat16)
    values = product(flip, mixed[:, 2 * width :].astype(jnp.bfloat16), 1, 0).astype(jnp.bfloat16)
    value_grad = jnp.zeros((length, width), jnp.float32)
    key_grad = jnp.zeros((length, width), jnp.float32)
    content_grad = jnp.zeros((length, width), jnp.float32)
    spread_grad = jnp.zeros((length, width), jnp.float32)
    table_grad = jnp.zeros((2 * length, width), jnp.float32)
    for head in range(head_count):
        mask = head_mask((length, width), head, head_size)
        head_grad = jnp.where(mask, grad, zero)
        value_grad += product(weights[head], head_grad, 0, 0)
        share = product(weights[head], flip, 1, 0)
        share_grad = product(head_grad, values, 1, 1)
        inner = jnp.sum(share * share_grad, axis=1, keepdims=True)
        score_grad = (share * (share_grad - inner)).astype(jnp.bfloat16).astype(jnp.float32)
        score_grad = score_grad * (1.0 / math.sqrt(head_size))
        low_grad = score_grad.astype(jnp.bfloat16)
        content_grad = jnp.where(mask, product(low_grad, keys, 1, 0), content_grad)
        key_grad += product(low_grad, jnp.where(mask, with_content[...], zero), 0, 0)
        wide = jnp.concatenate([score_grad, jnp.zeros((length, length), jnp.float32)], axis=1)
        shifted = pltpu.roll(wide, 0, 1, stride=1, stride_axis=0).astype(jnp.bfloat16)
        spread_grad = jnp.where(mask, product(shifted, reversed_position[...], 1, 0), spread_grad)
        table_grad += product(shifted, jnp.where(mask, with_position[...], zero), 0, 0)
    mixed_grad[:, :width] = (content_grad + spread_grad).astype(jnp.bfloat16)
    mixed_grad[:, width : 2 * width] = product(flip, key_grad.astype(jnp.bfloat16), 1, 0).astype(
        jnp.bfloat16
    )
    mixed_grad[:, 2 * width :] = value_grad.astype(jnp.bfloat16)
    position_grad[...] = table_grad.astype(jnp.bfloat16)
    bias_grad[0:1, :] = jnp.sum(content_grad, axis=0, keepdims=True)
    bias_grad[1:2, :] = jnp.sum(spread_grad, axis=0, keepdims=True)


def attend_back(grad, mixed, reversed_position, kept, head_count):
    length, width = grad.shape
    return pl.pallas_call(
        functools.partial(attend_back_kernel, head_count),
        out_shape=(
            jax.ShapeDtypeStruct((length, 3 * width), jnp.bfloat16),
            jax.ShapeDtypeStruct((2 * length, width), jnp.bfloat16),
            jax.ShapeDtypeStruct((2, width), jnp.float32),
        ),
        in_specs=[VMEM] * 6,
        out_specs=(VMEM,) * 3,
        compiler_params=pltpu.CompilerParams(vmem_limit_bytes=32 * 2**20),
        name="attend_back",
    )(grad, mixed, reversed_position, *kept)


def sum_after(piece, earlier):
    if earlier is not None:
        piece, _ = lax.optimization_barrier((piece, earlier))
    return lax.psum(piece, "dp")


def attention_front(values, gain_row, weight):
    normed = low(layer_norm(values, gain_row))
    return low_back(matmul(normed, weight))


def attention_back(attended, weight_out):
    return low_back(matmul(attended, weight_out))


def feed_forward(values, gain_row, weight_in, weight_out):
    normed = low(layer_norm(values, gain_row))
    hidden = low_back(matmul(normed, weight_in))
    active = low(jax.nn.silu(hidden))
    return low_back(matmul(active, weight_out))


def depthwise_conv(gated, kernel):
    half = kernel.shape[0] // 2
    return lax.conv_general_dilated(
        gated,
        kernel[:, None, :],
        (1,),
        [(half, half)],
        dimension_numbers=("NWC", "WIO", "NWC"),
        feature_group_count=gated.shape[2],
        precision=lax.Precision.HIGHEST,
    )


def conv_front(values, gain_row, weight_in, kernel):
    channels = kernel.shape[1]
    normed = low(layer_norm(values, gain_row))
    paired = low_back(matmul(normed, weight_in.reshape(weight_in.shape[0], 2 * channels))).reshape(
        -1, 2, channels
    )
    gated = paired[:, 0] * jax.nn.sigmoid(paired[:, 1])
    return depthwise_conv(gated.reshape(-1, LENGTH, channels), kernel)


def conv_back(mixed_rows, batch_mean, batch_var, scale_row, shift_row, weight_out):
    scaled = (mixed_rows - batch_mean) * lax.rsqrt(batch_var + EPS) * scale_row + shift_row
    swished = low(jax.nn.silu(scaled)).reshape(-1, mixed_rows.shape[2])
    return low_back(matmul(swished, weight_out))


def per_device(
    inputs,
    norm_gains,
    early_up,
    early_down,
    query_key_value,
    position_weight,
    position_bias,
    attention_out,
    pointwise_in,
    depthwise,
    batch_gain,
    batch_bias,
    pointwise_out,
    late_up,
    late_down,
    output_cotangent,
):
    stream = inputs.astype(jnp.float32)
    gain_rows = norm_gains.astype(jnp.float32)
    early_in = early_up.astype(jnp.float32)
    early_back = early_down.astype(jnp.float32)
    project_qkv = query_key_value.astype(jnp.float32)
    query_bias = position_bias.astype(jnp.float32)
    project_out = attention_out.astype(jnp.float32)
    point_first = pointwise_in.astype(jnp.float32)
    depth_taps = depthwise.astype(jnp.float32)
    scale_row = batch_gain.astype(jnp.float32)
    shift_row = batch_bias.astype(jnp.float32)
    point_second = pointwise_out.astype(jnp.float32)
    late_in = late_up.astype(jnp.float32)
    late_back = late_down.astype(jnp.float32)
    first_part, first_pull = jax.vjp(feed_forward, stream, gain_rows[0], early_in, early_back)
    after_first = tensor_sum(stream, first_part, 0.5, 0)

    model_width, _, local_width = project_qkv.shape
    head_count = query_bias.shape[1]
    table, reversed_table = sinusoid_tables(LENGTH, model_width)
    low_pos = position_weight
    position = product(table, low_pos, 1, 0).astype(jnp.bfloat16)
    reversed_position = product(reversed_table, low_pos, 1, 0).astype(jnp.bfloat16)
    bias_rows = query_bias.reshape(2, local_width)
    mixed_qkv, qkv_pull = jax.vjp(
        attention_front,
        after_first,
        gain_rows[1],
        project_qkv.reshape(model_width, 3 * local_width),
    )
    attended, *kept = attend(mixed_qkv, position, bias_rows, head_count)
    second_part, out_pull = jax.vjp(attention_back, attended.astype(jnp.float32), project_out)
    after_second = tensor_sum(after_first, second_part, 1.0, 1)
    mixed_rows, front_pull = jax.vjp(
        conv_front, after_second, gain_rows[2], point_first, depth_taps
    )
    token_count = mixed_rows.shape[0] * mixed_rows.shape[1] * lax.axis_size("dp")
    sum_values, sum_squares = exchange_many(
        (jnp.sum(mixed_rows, axis=(0, 1)), jnp.sum(mixed_rows * mixed_rows, axis=(0, 1))), "dp", 8
    )
    batch_mean = sum_values / token_count
    batch_var = sum_squares / token_count - batch_mean * batch_mean
    third_part, back_pull = jax.vjp(
        conv_back, mixed_rows, batch_mean, batch_var, scale_row, shift_row, point_second
    )
    after_third = tensor_sum(after_second, third_part, 1.0, 2)
    fourth_part, fourth_pull = jax.vjp(feed_forward, after_third, gain_rows[3], late_in, late_back)
    after_fourth = tensor_sum(after_third, fourth_part, 0.5, 3)
    result, final_pull = jax.vjp(layer_norm, after_fourth, gain_rows[4])
    grad_four, gain_five = final_pull(output_cotangent.astype(jnp.float32))
    cotangent_in, gain_four, late_in_grad, late_back_grad = fourth_pull(0.5 * grad_four)
    late_sum = sum_after(jnp.concatenate([late_in_grad, late_back_grad]), None)
    grad_three = tensor_sum(grad_four, cotangent_in, 1.0, 4)
    direct_grad, mean_grad, var_grad, scale_grad, shift_grad, second_point_grad = back_pull(
        grad_three
    )
    mean_grad, var_grad = exchange_many((mean_grad, var_grad), "dp", 9)
    mixed_grad = (
        direct_grad + (mean_grad + 2.0 * var_grad * (mixed_rows - batch_mean)) / token_count
    )
    cotangent_in, gain_three, first_point_grad, depth_grad = front_pull(mixed_grad)
    second_point_grad = sum_after(second_point_grad, late_sum)
    first_point_grad = sum_after(
        first_point_grad.reshape(model_width, 2 * local_width), second_point_grad
    )
    grad_two = tensor_sum(grad_three, cotangent_in, 1.0, 5)
    attended_grad, out_grad = out_pull(grad_two)
    qkv_grad, position_grad, bias_grad = attend_back(
        attended_grad.astype(jnp.bfloat16), mixed_qkv, reversed_position, kept, head_count
    )
    pos_grad = product(reversed_table, position_grad, 0, 0)
    cotangent_in, gain_two, qkv_grad = qkv_pull(qkv_grad.astype(jnp.float32))
    out_grad = sum_after(out_grad, first_point_grad)
    middle_sum = sum_after(jnp.concatenate([qkv_grad, pos_grad], axis=1), out_grad)
    grad_one = tensor_sum(grad_two, cotangent_in, 1.0, 6)
    cotangent_in, gain_one, early_in_grad, early_back_grad = first_pull(0.5 * grad_one)
    early_sum = sum_after(jnp.concatenate([early_in_grad, early_back_grad]), middle_sum)
    grad_zero = tensor_sum(grad_one, cotangent_in, 1.0, 7)
    (gain_grads,) = exchange_many(
        (jnp.stack([gain_one, gain_two, gain_three, gain_four]),), "tensor", 10
    )
    gain_grads, gain_five, bias_grad, depth_grad, scale_grad, shift_grad = exchange_many(
        (gain_grads, gain_five, bias_grad, depth_grad, scale_grad, shift_grad), "dp", 11
    )
    return (
        result.astype(jnp.bfloat16),
        grad_zero,
        jnp.concatenate([gain_grads, gain_five[None]]),
        early_sum[:model_width],
        early_sum[model_width:],
        middle_sum[:, : 3 * local_width].reshape(query_key_value.shape),
        middle_sum[:, 3 * local_width :],
        bias_grad.reshape(position_bias.shape),
        out_grad,
        first_point_grad.reshape(pointwise_in.shape),
        depth_grad,
        scale_grad,
        shift_grad,
        second_point_grad,
        late_sum[:model_width],
        late_sum[model_width:],
    )


def solution(mesh):
    return jax.shard_map(
        per_device,
        mesh=mesh,
        in_specs=(
            P("dp", None),
            P(),
            P(None, "tensor"),
            P("tensor", None),
            P(None, None, "tensor"),
            P(None, "tensor"),
            P(None, "tensor", None),
            P("tensor", None),
            P(None, None, "tensor"),
            P(None, "tensor"),
            P("tensor"),
            P("tensor"),
            P("tensor", None),
            P(None, "tensor"),
            P("tensor", None),
            P("dp", None),
        ),
        out_specs=(
            P("dp", None),
            P("dp", None),
            P(),
            P(None, "tensor"),
            P("tensor", None),
            P(None, None, "tensor"),
            P(None, "tensor"),
            P(None, "tensor", None),
            P("tensor", None),
            P(None, None, "tensor"),
            P(None, "tensor"),
            P("tensor"),
            P("tensor"),
            P("tensor", None),
            P(None, "tensor"),
            P("tensor", None),
        ),
        check_vma=False,
    )
```

time: 744 us -> 673 us (0.905)
  Pallas kernels: 0 us -> 171 us
  blocking collectives: 88.3 us -> 0 us
  local copies, waits for them, and re-layouts: 102 us -> 33.8 us
  other arithmetic: 75.2 us -> 30.1 us
  waiting for transfers between devices: 395 us -> 375 us
  matrix products: 56 us -> 39.6 us
    pallas_call x0 -> x14, Pallas kernels: none -> 171 us  [the longest x8 134 us: tensor_sum(): pl.pallas_call(functools.partial(tensor_kernel, factor, chunks), out_shap...]
    psum x4 -> x0, blocking collectives: 88.3 us -> none  [the longest x1 38.5 us: per_device(): lax.psum((gain_grads, early_in_grad, early_back_grad, qkv_grad, pos_grad,...]
    another operation x3 -> x1, other arithmetic: 34.7 us -> 0.02 us  [per_device(): jnp.stack([gain_one, gain_two, gain_three, gain_four])]
    reshape x8 -> x6, local copies, waits for them, and re-layouts: 36.3 us -> 2.33 us  [the longest x1 1.05 us: per_device(): first_point_grad.reshape(pointwise_in.shape)]
    psum x9 -> x6, waiting for transfers between devices: 394 us -> 375 us  [sum_after(): return lax.psum(piece, 'dp')]
    pad x4 -> x0, local copies, waits for them, and re-layouts: 9.85 us -> none  [the longest x2 6.36 us: relative_shift(): padded = jnp.pad(scores, ((0, 0), (0, 0), (1, 0)))]
    dot_general x27 -> x24, matrix products: 33.1 us -> 25 us  [matmul(): jnp.dot(first_factor, second_factor, preferred_element_type=jnp.float32)]
    slice x5 -> x10, local copies, waits for them, and re-layouts: 14.5 us -> 6.87 us  [the longest x1 3.08 us: per_device(): early_sum[model_width:]]
  transfers between devices with their start and end apart: 9 -> 6, of which waited for: 8 -> 6; matrix products, arithmetic and copies ran while one was open for 10% -> 7% of each run, Pallas kernels for 0% -> 14%
where the time goes in v1:
time: 673 us; the launch traced here: 667 us
  waiting for transfers between devices  375 us (56%)
  Pallas kernels  171 us (25%)
  matrix products  39.6 us (6%)
  local copies, waits for them, and re-layouts  33.8 us (5%)
  other arithmetic  30.1 us (4%)
  between operations  16.1 us (2%)
    psum x6, waiting for transfers between devices, sum_after(): return lax.psum(piece, 'dp')  375 us
    pallas_call x8, Pallas kernels, tensor_sum(): pl.pallas_call(functools.partial(tensor_kernel, factor, chunks), out_shap...  134 us
    pallas_call x4, Pallas kernels, exchange_sum(): pl.pallas_call(functools.partial(exchange_kernel, axis, count), out_shape...  30.2 us
    dot_general x24, matrix products, matmul(): jnp.dot(first_factor, second_factor, preferred_element_type=jnp.float32)  25 us
    unnamed x232, local copies, waits for them, and re-layouts  19.3 us
  transfers between devices with their start and end apart: 6, of which 6 were waited for; matrix products, arithmetic and copies ran while one was open for 7% of the time, Pallas kernels for 14%

profile of v1, /device:TPU:0, one launch (start us, length us, event | category | flops | bytes accessed | tf_op | source)
XLA Modules:
  0.0 666.5 jit_solution(2199101439064928499)
XLA Ops:
  14.7 17.7 %tensor_sum.8.base = f32[512,512]{1,0:T(8,128)S(1)} custom-call(f32[512,512]{1,0:T(8,128)S(1)} %fusion.49.part, f32[512,512]{1,0:T(8,128)S(1)} %convert_element_type.49.base), custom_call_target="tpu_custom_call" | custom-call | tf_op jit(solution)/shard_map/tensor_sum/pallas_call | solution.py:141
  36.1 3.0 attend.1
  41.6 16.8 %tensor_sum.9.base = f32[512,512]{1,0:T(8,128)S(1)} custom-call(f32[512,512]{1,0:T(8,128)S(1)} %fusion.51.part, f32[512,512]{1,0:T(8,128)S(1)} %tensor_sum.8.base), custom_call_target="tpu_custom_call" | custom-call | tf_op jit(solution)/shard_map/tensor_sum/pallas_call | solution.py:141
  66.1 2.9 fusion.41
  69.8 7.6 %exchange_dp.3 = f32[8,128]{1,0:T(8,128)S(1)} custom-call(f32[8,128]{1,0:T(8,128)S(1)} %maximum_maximum_fusion.part), custom_call_target="tpu_custom_call" | custom-call | tf_op jit(solution)/shard_map/exchange_dp/pallas_call | solution.py:203
  79.1 16.1 %tensor_sum.10.base = f32[512,512]{1,0:T(8,128)S(1)} custom-call(f32[512,512]{1,0:T(8,128)S(1)} %fusion.23.part, f32[512,512]{1,0:T(8,128)S(1)} %tensor_sum.9.base), custom_call_target="tpu_custom_call" | custom-call | tf_op jit(solution)/shard_map/tensor_sum/pallas_call | solution.py:141
  96.2 2.0 reduce_sum.293
  105.3 16.7 %tensor_sum.11 = f32[512,512]{1,0:T(8,128)S(1)} custom-call(f32[512,512]{1,0:T(8,128)S(1)} %fusion.52.part, f32[512,512]{1,0:T(8,128)S(1)} %copy-done.3), custom_call_target="tpu_custom_call" | custom-call | tf_op jit(solution)/shard_map/tensor_sum/pallas_call | solution.py:141
  123.0 2.0 reduce_sum.295
  127.5 2.2 fusion.3
  135.5 2.7 multiply_reduce_fusion
  139.5 16.8 %tensor_sum.12.base = f32[512,512]{1,0:T(8,128)S(1)} custom-call(f32[512,512]{1,0:T(8,128)S(1)} %broadcast_add_fusion.3.part, f32[512,512]{1,0:T(8,128)S(1)} %copy-done.9), custom_call_target="tpu_custom_call" | custom-call | tf_op jit(solution)/shard_map/tensor_sum/pallas_call | solution.py:141
  157.4 7.4 %exchange_dp.4 = f32[8,128]{1,0:T(8,128)S(1)} custom-call(f32[8,128]{1,0:T(8,128)S(1)} %maximum_maximum_fusion.1.part), custom_call_target="tpu_custom_call" | custom-call | tf_op jit(solution)/shard_map/exchange_dp/pallas_call | solution.py:203
  165.6 2.0 fusion.25
  167.6 1.8 copy.75
  172.5 16.7 %tensor_sum.13.base = f32[512,512]{1,0:T(8,128)S(1)} custom-call(f32[512,512]{1,0:T(8,128)S(1)} %broadcast_add_fusion.2.part, f32[512,512]{1,0:T(8,128)S(1)} %copy-done.8), custom_call_target="tpu_custom_call" | custom-call | tf_op jit(solution)/shard_map/tensor_sum/pallas_call | solution.py:141
  190.5 3.8 attend_back.1
  195.6 16.8 %tensor_sum.14.base = f32[512,512]{1,0:T(8,128)S(1)} custom-call(f32[512,512]{1,0:T(8,128)S(1)} %broadcast_add_fusion.1.part, f32[512,512]{1,0:T(8,128)S(1)} %tensor_sum.13.base), custom_call_target="tpu_custom_call" | custom-call | tf_op jit(solution)/shard_map/tensor_sum/pallas_call | solution.py:141
  213.5 3.0 fusion.9
  216.5 21.8 %all-reduce.9.cloned.1.call-done = f32[1024,512]{1,0:T(8,128)} async-done(((f32[1024,512]{1,0:T(8,128)}), f32[1024,512]{1,0:T(8,128)}) %all-reduce.9.cloned.1.call-update) | async-done | bytes 2097168 | tf_op jit(solution)/shard_map/psum | solution.py:373
  239.7 2.1 fusion.58
  241.8 70.8 %all-reduce.11.cloned.1.call-done = f32[128,512]{1,0:T(8,128)} async-done(((f32[128,512]{1,0:T(8,128)}), f32[128,512]{1,0:T(8,128)}) %all-reduce.11.cloned.1.call-update) | async-done | bytes 262160 | tf_op jit(solution)/shard_map/psum | solution.py:373
  316.3 72.3 %all-reduce.13.cloned.1.call-done = f32[512,256]{1,0:T(8,128)} async-done(((f32[512,256]{1,0:T(8,128)}), f32[512,256]{1,0:T(8,128)}) %all-reduce.13.cloned.1.call-update) | async-done | bytes 524304 | tf_op jit(solution)/shard_map/psum | solution.py:373
  390.2 72.1 %all-reduce.15.cloned.1.call-done = f32[128,512]{1,0:T(8,128)} async-done(((f32[128,512]{1,0:T(8,128)}), f32[128,512]{1,0:T(8,128)}) %all-reduce.15.cloned.1.call-update) | async-done | bytes 262160 | tf_op jit(solution)/shard_map/psum | solution.py:373
  468.0 76.1 %all-reduce.17.cloned.1.call-done = f32[512,512]{0,1:T(8,128)} async-done(((f32[512,512]{0,1:T(8,128)}), f32[512,512]{0,1:T(8,128)}) %all-reduce.17.cloned.1.call-update) | async-done | bytes 1048592 | tf_op jit(solution)/shard_map/psum | solution.py:373
  544.1 4.0 exchange_tensor.1
  548.2 5.9 fusion.48
  554.4 11.2 %exchange_dp.5 = f32[56,128]{1,0:T(8,128)S(1)} custom-call(f32[56,128]{1,0:T(8,128)S(1)} %concatenate.23.part), custom_call_target="tpu_custom_call" | custom-call | tf_op jit(solution)/shard_map/exchange_dp/pallas_call | solution.py:203
  566.6 16.8 %tensor_sum.15 = f32[512,512]{1,0:T(8,128)S(1)} custom-call(f32[512,512]{1,0:T(8,128)S(1)} %broadcast_add_fusion.part, f32[512,512]{1,0:T(8,128)S(1)} %tensor_sum.14.base), custom_call_target="tpu_custom_call" | custom-call | tf_op jit(solution)/shard_map/tensor_sum/pallas_call | solution.py:141
  585.2 3.1 fusion.45
  591.4 62.2 %all-reduce.19.cloned.1.call-done = f32[1024,512]{1,0:T(8,128)} async-done(((f32[1024,512]{1,0:T(8,128)}), f32[1024,512]{1,0:T(8,128)}) %all-reduce.19.cloned.1.call-update) | async-done | bytes 2097168 | tf_op jit(solution)/shard_map/psum | solution.py:373
  653.6 3.1 fusion.46
  (352 shorter events, 71.1 us)
Async XLA Ops:
  7.2 95.1 %copy-start = (bf16[512,512]{1,0:T(8,128)(2,1)S(1)}, bf16[512,512]{1,0:T(8,128)(2,1)}, u32[]{:S(2)}) copy-start(bf16[512,512]{1,0:T(8,128)(2,1)} %param.31) | copy-start | bytes 1572868
  7.2 231.0 %all-reduce.9.cloned.1.call-start = ((), (), s32[]{:S(2)}) async-start(), calls=%async_computation | async-start | bytes 4194304 | tf_op jit(solution)/shard_map/psum | solution.py:373
  11.3 21.6 %copy-start.72 = (f32[1,512]{1,0:T(1,128)}, f32[1,512]{1,0:T(1,128)S(1)}, u32[]{:S(2)}) copy-start(f32[1,512]{1,0:T(1,128)S(1)} %get-tuple-element.126) | copy-start | bytes 6148
  34.0 7.4 %copy-start.51 = (bf16[128,512]{1,0:T(8,128)(2,1)S(1)}, bf16[128,512]{1,0:T(8,128)(2,1)}, u32[]{:S(2)}) copy-start(bf16[128,512]{1,0:T(8,128)(2,1)} %param.25) | copy-start | bytes 393220
  66.1 11.3 %copy-start.109 = (bf16[128]{0:T(256)(128)(2,1)S(1)}, bf16[128]{0:T(256)(128)(2,1)}, u32[]{:S(2)}) copy-start(bf16[128]{0:T(256)(128)(2,1)} %param.29) | copy-start | bytes 772
  66.1 11.3 %copy-start.110 = (bf16[128]{0:T(256)(128)(2,1)S(1)}, bf16[128]{0:T(256)(128)(2,1)}, u32[]{:S(2)}) copy-start(bf16[128]{0:T(256)(128)(2,1)} %param.28) | copy-start | bytes 772
  66.1 12.7 %copy-start.65 = (bf16[128,512]{1,0:T(8,128)(2,1)S(1)}, bf16[128,512]{1,0:T(8,128)(2,1)}, u32[]{:S(2)}) copy-start(bf16[128,512]{1,0:T(8,128)(2,1)} %param.30) | copy-start | bytes 393220
  69.0 8.4 %copy-start.48 = (f32[1,512,128]{2,0,1:T(1,128)}, f32[1,512,128]{2,0,1:T(1,128)S(1)}, u32[]{:S(2)}) copy-start(f32[1,512,128]{2,0,1:T(1,128)S(1)} %get-tuple-element.134) | copy-start | bytes 786436
  135.4 177.2 %all-reduce.11.cloned.1.call-start = ((), (), s32[]{:S(2)}) async-start(), calls=%async_computation.1 | async-start | bytes 524288 | tf_op jit(solution)/shard_map/psum | solution.py:373
  139.4 16.9 %copy-start.49 = (f32[1,512,128]{2,0,1:T(1,128)S(1)}, f32[1,512,128]{2,0,1:T(1,128)}, u32[]{:S(2)}) copy-start(f32[1,512,128]{2,0,1:T(1,128)} %copy-done.48) | copy-start | bytes 786436
  139.4 16.9 %copy-start.66 = (bf16[128,512]{1,0:T(8,128)(2,1)S(1)}, bf16[128,512]{1,0:T(8,128)(2,1)}, u32[]{:S(2)}) copy-start(bf16[128,512]{1,0:T(8,128)(2,1)} %param.30) | copy-start | bytes 393220
  139.4 16.9 %copy-start.98 = (f32[128]{0:T(128)S(1)}, f32[128]{0:T(128)}, u32[]{:S(2)}) copy-start(f32[128]{0:T(128)} %copy-done.97) | copy-start | bytes 1540
  139.4 16.9 %copy-start.100 = (f32[128]{0:T(128)S(1)}, f32[128]{0:T(128)}, u32[]{:S(2)}) copy-start(f32[128]{0:T(128)} %copy-done.99) | copy-start | bytes 1540
  139.4 16.9 %copy-start.102 = (f32[128]{0:T(128)S(1)}, f32[128]{0:T(128)}, u32[]{:S(2)}) copy-start(f32[128]{0:T(128)} %copy-done.101) | copy-start | bytes 1540
  139.4 16.9 %copy-start.107 = (f32[128]{0:T(128)S(1)}, f32[128]{0:T(128)}, u32[]{:S(2)}) copy-start(f32[128]{0:T(128)} %copy-done.106) | copy-start | bytes 1540
  156.4 9.2 %copy-start.108 = (bf16[31,128]{1,0:T(8,128)(2,1)S(1)}, bf16[31,128]{1,0:T(8,128)(2,1)}, u32[]{:S(2)}) copy-start(bf16[31,128]{1,0:T(8,128)(2,1)} %param.27) | copy-start | bytes 23812
  172.5 16.8 %copy-start.52 = (bf16[128,512]{1,0:T(8,128)(2,1)S(1)}, bf16[128,512]{1,0:T(8,128)(2,1)}, u32[]{:S(2)}) copy-start(bf16[128,512]{1,0:T(8,128)(2,1)} %param.25) | copy-start | bytes 393220
  172.5 17.1 %copy-start.27 = (bf16[1024,512]{1,0:T(8,128)(2,1)S(1)}, bf16[1024,512]{1,0:T(8,128)(2,1)}, u32[]{:S(2)}) copy-start(bf16[1024,512]{1,0:T(8,128)(2,1)} %constant.58.clone) | copy-start | bytes 3145732
  172.5 17.2 %copy-start.58 = (bf16[512,128]{1,0:T(8,128)(2,1)S(1)}, bf16[512,128]{1,0:T(8,128)(2,1)}, u32[]{:S(2)}) copy-start(bf16[512,128]{1,0:T(8,128)(2,1)} %param.23) | copy-start | bytes 393220
  195.5 16.9 %copy-start.33 = (bf16[512,512]{1,0:T(8,128)(2,1)S(1)}, bf16[512,512]{1,0:T(8,128)(2,1)}, u32[]{:S(2)}) copy-start(bf16[512,512]{1,0:T(8,128)(2,1)} %copy-done.32) | copy-start | bytes 1572868
  195.6 16.9 %copy-start.44 = (bf16[1,512,128]{2,1,0:T(8,128)(2,1)S(1)}, bf16[1,512,128]{2,1,0:T(8,128)(2,1)}, u32[]{:S(2)}) copy-start(bf16[1,512,128]{2,1,0:T(8,128)(2,1)} %copy-done.43) | copy-start | bytes 393220
  213.5 24.9 %copy-start.22 = (bf16[512,512]{1,0:T(8,128)(2,1)S(1)}, bf16[512,512]{1,0:T(8,128)(2,1)}, u32[]{:S(2)}) copy-start(bf16[512,512]{1,0:T(8,128)(2,1)} %copy-done.21) | copy-start | bytes 1572868
  216.5 23.2 %copy-start.24 = (bf16[512,512]{1,0:T(8,128)(2,1)S(1)}, bf16[512,512]{1,0:T(8,128)(2,1)}, u32[]{:S(2)}) copy-start(bf16[512,512]{1,0:T(8,128)(2,1)} %copy-done.23) | copy-start | bytes 1572868
  216.5 96.2 %copy-start.13 = (bf16[1024,128]{1,0:T(8,128)(2,1)S(1)}, bf16[1024,128]{1,0:T(8,128)(2,1)}, u32[]{:S(2)}) copy-start(bf16[1024,128]{1,0:T(8,128)(2,1)} %copy-done.12) | copy-start | bytes 786436
  238.3 150.3 %all-reduce.13.cloned.1.call-start = ((), (), s32[]{:S(2)}) async-start(), calls=%async_computation.2 | async-start | bytes 1048576 | tf_op jit(solution)/shard_map/psum | solution.py:373
  312.6 149.7 %all-reduce.15.cloned.1.call-start = ((), (), s32[]{:S(2)}) async-start(), calls=%async_computation.3 | async-start | bytes 524288 | tf_op jit(solution)/shard_map/psum | solution.py:373
  314.3 74.4 %copy-start.35 = (bf16[512,512]{1,0:T(8,128)(2,1)S(1)}, bf16[512,512]{1,0:T(8,128)(2,1)}, u32[]{:S(2)}) copy-start(bf16[512,512]{1,0:T(8,128)(2,1)} %copy-done.34) | copy-start | bytes 1572868
  388.7 155.4 %all-reduce.17.cloned.1.call-start = ((), (), s32[]{:S(2)}) async-start(), calls=%async_computation.4 | async-start | bytes 2097152 | tf_op jit(solution)/shard_map/psum | solution.py:373
  462.3 191.3 %all-reduce.19.cloned.1.call-start = ((), (), s32[]{:S(2)}) async-start(), calls=%async_computation.5 | async-start | bytes 4194304 | tf_op jit(solution)/shard_map/psum | solution.py:373
  467.3 76.7 %copy-start.94 = (f32[512]{0:T(512)S(1)}, f32[512]{0:T(512)}, u32[]{:S(2)}) copy-start(f32[512]{0:T(512)} %get-tuple-element.92) | copy-start | bytes 6148
  467.3 80.8 %copy-start.60 = (f32[1,512,128]{2,0,1:T(1,128)S(1)}, f32[1,512,128]{2,0,1:T(1,128)}, u32[]{:S(2)}) copy-start(f32[1,512,128]{2,0,1:T(1,128)} %copy.69) | copy-start | bytes 786436
  467.3 80.8 %copy-start.64 = (f32[1,512,128]{2,1,0:T(8,128)S(1)}, f32[1,512,128]{2,1,0:T(8,128)}, u32[]{:S(2)}) copy-start(f32[1,512,128]{2,1,0:T(8,128)} %copy-done.63) | copy-start | bytes 786436
  (88 other events, 189.6 us)
Sparse Core Ops, SparseCore 0:
  135.5 102.7 all-reduce.8
  242.2 70.2 all-reduce.10
  316.9 71.6 all-reduce.12
  392.4 69.8 all-reduce.14
  466.6 77.3 all-reduce.16
  547.5 106.0 all-reduce.18

commit v2 on v1

--- a/solution.py
+++ b/solution.py
@@ -367,10 +367,106 @@
     )(grad, mixed, reversed_position, *kept)
 
 
-def sum_after(piece, earlier):
-    if earlier is not None:
-        piece, _ = lax.optimization_barrier((piece, earlier))
-    return lax.psum(piece, "dp")
+def halving_kernel(count, groups, part, out, work, land, send, recv):
+    me = lax.axis_index("dp")
+    bits = [1 << k for k in range(count.bit_length() - 1)]
+    orders = [bits, bits[1:] + bits[:1]]
+    stages = len(bits)
+    height = part.shape[0] // groups
+    barrier = pltpu.get_barrier_semaphore()
+
+    def side(bit):
+        return lax.rem(me // bit, 2)
+
+    def partner(bit):
+        return me + bit * (1 - 2 * side(bit))
+
+    for bit in bits:
+        pl.semaphore_signal(barrier, inc=1, device_id={"dp": partner(bit)}, device_id_type=MESH)
+    pl.semaphore_wait(barrier, stages)
+
+    def span(start, size):
+        return pl.ds(pl.multiple_of(start, 8), size)
+
+    spans = []
+    for group in range(groups):
+        start = group * height
+        steps = []
+        for k, bit in enumerate(orders[group % 2]):
+            size = height >> (k + 1)
+            keep = start + side(bit) * size
+            give = start + (1 - side(bit)) * size
+            steps.append((bit, span(keep, size), span(give, size)))
+            start = keep
+        spans.append(steps)
+
+    def landing(group, k):
+        return pl.ds(group * height + height - (height >> k), height >> (k + 1))
+
+    def remote(source, target, group, stage, bit):
+        return pltpu.make_async_remote_copy(
+            src_ref=source,
+            dst_ref=target,
+            send_sem=send.at[group, stage],
+            recv_sem=recv.at[group, stage],
+            device_id={"dp": partner(bit)},
+            device_id_type=MESH,
+        )
+
+    def down(group, k):
+        bit, _, give = spans[group][k]
+        source = part if k == 0 else work
+        return remote(source.at[give], land.at[landing(group, k)], group, k, bit)
+
+    def up(group, k):
+        bit, keep, _ = spans[group][k]
+        return remote(out.at[keep], out.at[keep], group, stages + k, bit)
+
+    for group in range(groups):
+        down(group, 0).start()
+    for k in range(stages):
+        for group in range(groups):
+            keep = spans[group][k][1]
+            source = part if k == 0 else work
+            down(group, k).wait_recv()
+            total = source[keep, :] + land[landing(group, k), :]
+            if k < stages - 1:
+                work[keep, :] = total
+                down(group, k + 1).start()
+            else:
+                out[keep, :] = total
+                up(group, k).start()
+    for k in reversed(range(stages)):
+        for group in range(groups):
+            up(group, k).wait_recv()
+            if k > 0:
+                up(group, k - 1).start()
+    for group in range(groups):
+        for k in range(stages):
+            down(group, k).wait_send()
+            up(group, k).wait_send()
+
+
+def halving_sum(part, ident, groups=4):
+    count = lax.axis_size("dp")
+    stages = count.bit_length() - 1
+    buffer = pltpu.VMEM(part.shape, jnp.float32)
+    return pl.pallas_call(
+        functools.partial(halving_kernel, count, groups),
+        out_shape=jax.ShapeDtypeStruct(part.shape, jnp.float32),
+        in_specs=[VMEM],
+        out_specs=VMEM,
+        scratch_shapes=[
+            buffer,
+            buffer,
+            pltpu.SemaphoreType.DMA((groups, 2 * stages)),
+            pltpu.SemaphoreType.DMA((groups, 2 * stages)),
+        ],
+        compiler_params=pltpu.CompilerParams(
+            collective_id=ident, has_side_effects=True, vmem_limit_bytes=32 * 2**20
+        ),
+        name="halving_sum",
+    )(part)
 
 
 def attention_front(values, gain_row, weight):
@@ -487,7 +583,7 @@
     result, final_pull = jax.vjp(layer_norm, after_fourth, gain_rows[4])
     grad_four, gain_five = final_pull(output_cotangent.astype(jnp.float32))
     cotangent_in, gain_four, late_in_grad, late_back_grad = fourth_pull(0.5 * grad_four)
-    late_sum = sum_after(jnp.concatenate([late_in_grad, late_back_grad]), None)
+    late_in_grad, late_back_grad = lax.psum((late_in_grad, late_back_grad), "dp")
     grad_three = tensor_sum(grad_four, cotangent_in, 1.0, 4)
     direct_grad, mean_grad, var_grad, scale_grad, shift_grad, second_point_grad = back_pull(
         grad_three
@@ -497,10 +593,6 @@
         direct_grad + (mean_grad + 2.0 * var_grad * (mixed_rows - batch_mean)) / token_count
     )
     cotangent_in, gain_three, first_point_grad, depth_grad = front_pull(mixed_grad)
-    second_point_grad = sum_after(second_point_grad, late_sum)
-    first_point_grad = sum_after(
-        first_point_grad.reshape(model_width, 2 * local_width), second_point_grad
-    )
     grad_two = tensor_sum(grad_three, cotangent_in, 1.0, 5)
     attended_grad, out_grad = out_pull(grad_two)
     qkv_grad, position_grad, bias_grad = attend_back(
@@ -508,11 +600,25 @@
     )
     pos_grad = product(reversed_table, position_grad, 0, 0)
     cotangent_in, gain_two, qkv_grad = qkv_pull(qkv_grad.astype(jnp.float32))
-    out_grad = sum_after(out_grad, first_point_grad)
-    middle_sum = sum_after(jnp.concatenate([qkv_grad, pos_grad], axis=1), out_grad)
     grad_one = tensor_sum(grad_two, cotangent_in, 1.0, 6)
     cotangent_in, gain_one, early_in_grad, early_back_grad = first_pull(0.5 * grad_one)
-    early_sum = sum_after(jnp.concatenate([early_in_grad, early_back_grad]), middle_sum)
+    first_point_grad = first_point_grad.reshape(model_width, 2 * local_width)
+    fold = model_width // 2
+    pieces = (
+        early_in_grad,
+        early_back_grad,
+        jnp.concatenate([qkv_grad, pos_grad], axis=1),
+        jnp.concatenate([first_point_grad[:fold], first_point_grad[fold:]], axis=1),
+        out_grad,
+        second_point_grad,
+    )
+    summed = halving_sum(jnp.concatenate(pieces), 12)
+    early_in_grad, early_back_grad, middle_sum, first_sum, out_grad, second_point_grad = jnp.split(
+        summed, np.cumsum([piece.shape[0] for piece in pieces])[:-1].tolist()
+    )
+    first_point_grad = jnp.concatenate(
+        [first_sum[:, : 2 * local_width], first_sum[:, 2 * local_width :]]
+    )
     grad_zero = tensor_sum(grad_one, cotangent_in, 1.0, 7)
     (gain_grads,) = exchange_many(
         (jnp.stack([gain_one, gain_two, gain_three, gain_four]),), "tensor", 10
@@ -524,8 +630,8 @@
         result.astype(jnp.bfloat16),
         grad_zero,
         jnp.concatenate([gain_grads, gain_five[None]]),
-        early_sum[:model_width],
-        early_sum[model_width:],
+        early_in_grad,
+        early_back_grad,
         middle_sum[:, : 3 * local_width].reshape(query_key_value.shape),
         middle_sum[:, 3 * local_width :],
         bias_grad.reshape(position_bias.shape),
@@ -535,8 +641,8 @@
         scale_grad,
         shift_grad,
         second_point_grad,
-        late_sum[:model_width],
-        late_sum[model_width:],
+        late_in_grad,
+        late_back_grad,
     )
 
 

time: 673 us -> 417 us (0.62)
  waiting for transfers between devices: 375 us -> 0.02 us
  Pallas kernels: 171 us -> 283 us
    psum x6 -> x1, waiting for transfers between devices: 375 us -> 0.01 us  [per_device(): lax.psum((late_in_grad, late_back_grad), 'dp')]
    pallas_call x0 -> x1, Pallas kernels: none -> 114 us  [halving_sum(): pl.pallas_call(functools.partial(halving_kernel, count, groups), out_shap...]
    unnamed x232 -> x199, local copies, waits for them, and re-layouts: 19.3 us -> 19.8 us
  transfers between devices with their start and end apart: 6 -> 1, of which waited for: 6 -> 0; matrix products, arithmetic and copies ran while one was open for 7% -> 12% of each run, Pallas kernels for 14% -> 50%
where the time goes in v2:
time: 417 us; the launch traced here: 409 us
  Pallas kernels  283 us (68%)
  matrix products  39.2 us (9%)
  local copies, waits for them, and re-layouts  38.1 us (9%)
  other arithmetic  33.6 us (8%)
  between operations  15.8 us (4%)
    pallas_call x8, Pallas kernels, tensor_sum(): pl.pallas_call(functools.partial(tensor_kernel, factor, chunks), out_shap...  134 us
    pallas_call x1, Pallas kernels, halving_sum(): pl.pallas_call(functools.partial(halving_kernel, count, groups), out_shap...  114 us
    pallas_call x4, Pallas kernels, exchange_sum(): pl.pallas_call(functools.partial(exchange_kernel, axis, count), out_shape...  28.2 us
    dot_general x24, matrix products, matmul(): jnp.dot(first_factor, second_factor, preferred_element_type=jnp.float32)  24.7 us
    unnamed x199, local copies, waits for them, and re-layouts  19.8 us
    conv_general_dilated x3, matrix products, depthwise_conv(): lax.conv_general_dilated(gated, kernel[:, None, :], (1,), [(half, half)],...  12 us
    reduce_sum x8, other arithmetic, layer_norm(): centre = values - jnp.mean(values, axis=-1, keepdims=True)  8.59 us
  transfers between devices with their start and end apart: 1, of which 0 were waited for; matrix products, arithmetic and copies ran while one was open for 12% of the time, Pallas kernels for 50%

profile of v2, /device:TPU:0, one launch (start us, length us, event | category | flops | bytes accessed | tf_op | source)
XLA Modules:
  0.0 409.3 jit_solution(7794790363865669272)
XLA Ops:
  18.6 17.7 %tensor_sum.8.base = f32[512,512]{1,0:T(8,128)S(1)} custom-call(f32[512,512]{1,0:T(8,128)S(1)} %fusion.50.part, f32[512,512]{1,0:T(8,128)S(1)} %convert_element_type.49.base), custom_call_target="tpu_custom_call" | custom-call | tf_op jit(solution)/shard_map/tensor_sum/pallas_call | solution.py:141
  37.9 1.6 convolution_convert_fusion.1.position
  39.6 3.0 attend.1
  46.0 16.8 %tensor_sum.9.base = f32[512,512]{1,0:T(8,128)S(1)} custom-call(f32[512,512]{1,0:T(8,128)S(1)} %fusion.52.part, f32[512,512]{1,0:T(8,128)S(1)} %tensor_sum.8.base), custom_call_target="tpu_custom_call" | custom-call | tf_op jit(solution)/shard_map/tensor_sum/pallas_call | solution.py:141
  69.6 1.8 copy.76
  71.4 3.3 fusion.40
  75.4 7.6 %exchange_dp.3 = f32[8,128]{1,0:T(8,128)S(1)} custom-call(f32[8,128]{1,0:T(8,128)S(1)} %maximum_maximum_fusion.part), custom_call_target="tpu_custom_call" | custom-call | tf_op jit(solution)/shard_map/exchange_dp/pallas_call | solution.py:203
  84.7 16.2 %tensor_sum.10.base = f32[512,512]{1,0:T(8,128)S(1)} custom-call(f32[512,512]{1,0:T(8,128)S(1)} %fusion.22.part, f32[512,512]{1,0:T(8,128)S(1)} %tensor_sum.9.base), custom_call_target="tpu_custom_call" | custom-call | tf_op jit(solution)/shard_map/tensor_sum/pallas_call | solution.py:141
  101.8 2.0 reduce_sum.293
  110.8 16.8 %tensor_sum.11 = f32[512,512]{1,0:T(8,128)S(1)} custom-call(f32[512,512]{1,0:T(8,128)S(1)} %fusion.53.part, f32[512,512]{1,0:T(8,128)S(1)} %copy-done.3), custom_call_target="tpu_custom_call" | custom-call | tf_op jit(solution)/shard_map/tensor_sum/pallas_call | solution.py:141
  128.5 2.0 reduce_sum.295
  131.2 1.9 fusion.2
  133.1 2.5 fusion.3
  135.6 3.0 multiply_convert_fusion.1
  143.1 2.7 multiply_reduce_fusion
  146.5 1.6 fusion.43
  148.4 16.8 %tensor_sum.12.base = f32[512,512]{1,0:T(8,128)S(1)} custom-call(f32[512,512]{1,0:T(8,128)S(1)} %broadcast_add_fusion.3.part, f32[512,512]{1,0:T(8,128)S(1)} %copy-done.8), custom_call_target="tpu_custom_call" | custom-call | tf_op jit(solution)/shard_map/tensor_sum/pallas_call | solution.py:141
  166.3 7.4 %exchange_dp.4 = f32[8,128]{1,0:T(8,128)S(1)} custom-call(f32[8,128]{1,0:T(8,128)S(1)} %maximum_maximum_fusion.1.part), custom_call_target="tpu_custom_call" | custom-call | tf_op jit(solution)/shard_map/exchange_dp/pallas_call | solution.py:203
  173.9 6.5 %fusion.49 = f32[31,1,128]{2,1,0:T(1,128)} fusion(f32[1,512,128]{2,0,1:T(1,128)S(1)} %copy-done.52, f32[1,512,128]{2,0,1:T(1,128)S(1)} %bitcast.146), kind=kOutput, calls=%fused_computation.149 | convolution fusion | flops 24010752 | bytes 540160 | tf_op jit(solution)/shard_map/transpose(jvp())/conv_general_dilated | solution.py:490
  180.4 2.2 fusion.24
  182.6 1.8 copy.82
  187.9 16.8 %tensor_sum.13.base = f32[512,512]{1,0:T(8,128)S(1)} custom-call(f32[512,512]{1,0:T(8,128)S(1)} %broadcast_add_fusion.2.part, f32[512,512]{1,0:T(8,128)S(1)} %copy-done.7), custom_call_target="tpu_custom_call" | custom-call | tf_op jit(solution)/shard_map/tensor_sum/pallas_call | solution.py:141
  205.5 3.8 attend_back.1
  210.6 16.8 %tensor_sum.14.base = f32[512,512]{1,0:T(8,128)S(1)} custom-call(f32[512,512]{1,0:T(8,128)S(1)} %broadcast_add_fusion.1.part, f32[512,512]{1,0:T(8,128)S(1)} %tensor_sum.13.base), custom_call_target="tpu_custom_call" | custom-call | tf_op jit(solution)/shard_map/tensor_sum/pallas_call | solution.py:141
  237.1 3.8 exchange_tensor.1
  241.1 9.4 %exchange_dp.5 = f32[56,128]{1,0:T(8,128)S(1)} custom-call(f32[56,128]{1,0:T(8,128)S(1)} %concatenate.26.part), custom_call_target="tpu_custom_call" | custom-call | tf_op jit(solution)/shard_map/exchange_dp/pallas_call | solution.py:203
  250.6 2.0 convolution_dynamic-update-slice_fusion.2.part
  252.6 113.6 %halving_sum.1 = f32[2048,512]{1,0:T(8,128)S(1)} custom-call(f32[2048,512]{1,0:T(8,128)} %convolution_dynamic-update-slice_fusion.2.part), custom_call_target="tpu_custom_call" | custom-call | tf_op jit(solution)/shard_map/halving_sum/pallas_call | solution.py:454
  370.2 16.3 %tensor_sum.15 = f32[512,512]{1,0:T(8,128)S(1)} custom-call(f32[512,512]{1,0:T(8,128)S(1)} %broadcast_add_fusion.part, f32[512,512]{1,0:T(8,128)S(1)} %tensor_sum.14.base), custom_call_target="tpu_custom_call" | custom-call | tf_op jit(solution)/shard_map/tensor_sum/pallas_call | solution.py:141
  393.0 1.9 fusion.44
  394.9 3.1 fusion.46
  398.9 2.3 copy.132
  (308 shorter events, 69.0 us)
Async XLA Ops:
  7.2 100.8 %copy-start = (bf16[512,512]{1,0:T(8,128)(2,1)S(1)}, bf16[512,512]{1,0:T(8,128)(2,1)}, u32[]{:S(2)}) copy-start(bf16[512,512]{1,0:T(8,128)(2,1)} %param.31) | copy-start | bytes 1572868
  7.2 390.8 %all-reduce.5.cloned.1.call-start = ((), (), s32[]{:S(2)}) async-start(), calls=%async_computation | async-start | bytes 4194304 | tf_op jit(solution)/shard_map/psum | solution.py:586
  13.1 23.6 %copy-start.58 = (f32[1,512]{1,0:T(1,128)}, f32[1,512]{1,0:T(1,128)S(1)}, u32[]{:S(2)}) copy-start(f32[1,512]{1,0:T(1,128)S(1)} %get-tuple-element.122) | copy-start | bytes 6148
  18.1 18.9 %copy-start.51 = (bf16[512,3,128]{2,0,1:T(8,128)(2,1)S(1)}, bf16[512,3,128]{2,0,1:T(8,128)(2,1)}, u32[]{:S(2)}) copy-start(bf16[512,3,128]{2,0,1:T(8,128)(2,1)} %param.22) | copy-start | bytes 1179652
  18.5 18.6 %copy-start.86 = (bf16[2,2,64]{2,1,0:T(2,128)(2,1)S(1)}, bf16[2,2,64]{2,1,0:T(2,128)(2,1)}, u32[]{:S(2)}) copy-start(bf16[2,2,64]{2,1,0:T(2,128)(2,1)} %param.24) | copy-start | bytes 1540
  18.5 19.4 %copy-start.49 = (bf16[512,128]{1,0:T(8,128)(2,1)S(1)}, bf16[512,128]{1,0:T(8,128)(2,1)}, u32[]{:S(2)}) copy-start(bf16[512,128]{1,0:T(8,128)(2,1)} %param.23) | copy-start | bytes 393220
  71.4 13.0 %copy-start.53 = (bf16[128,512]{1,0:T(8,128)(2,1)S(1)}, bf16[128,512]{1,0:T(8,128)(2,1)}, u32[]{:S(2)}) copy-start(bf16[128,512]{1,0:T(8,128)(2,1)} %param.30) | copy-start | bytes 393220
  148.1 17.1 %copy-start.39 = (f32[1,512,128]{2,0,1:T(1,128)S(1)}, f32[1,512,128]{2,0,1:T(1,128)}, u32[]{:S(2)}) copy-start(f32[1,512,128]{2,0,1:T(1,128)} %copy-done.38) | copy-start | bytes 786436
  148.1 17.1 %copy-start.54 = (bf16[128,512]{1,0:T(8,128)(2,1)S(1)}, bf16[128,512]{1,0:T(8,128)(2,1)}, u32[]{:S(2)}) copy-start(bf16[128,512]{1,0:T(8,128)(2,1)} %param.30) | copy-start | bytes 393220
  148.1 17.1 %copy-start.81 = (f32[128]{0:T(128)S(1)}, f32[128]{0:T(128)}, u32[]{:S(2)}) copy-start(f32[128]{0:T(128)} %copy-done.80) | copy-start | bytes 1540
  148.2 17.1 %copy-start.83 = (f32[128]{0:T(128)S(1)}, f32[128]{0:T(128)}, u32[]{:S(2)}) copy-start(f32[128]{0:T(128)} %copy-done.82) | copy-start | bytes 1540
  148.2 17.1 %copy-start.85 = (f32[128]{0:T(128)S(1)}, f32[128]{0:T(128)}, u32[]{:S(2)}) copy-start(f32[128]{0:T(128)} %copy-done.84) | copy-start | bytes 1540
  148.2 17.1 %copy-start.90 = (f32[128]{0:T(128)S(1)}, f32[128]{0:T(128)}, u32[]{:S(2)}) copy-start(f32[128]{0:T(128)} %copy-done.89) | copy-start | bytes 1540
  148.3 17.9 %copy-start.79 = (f32[8]{0:T(128)S(1)}, f32[8]{0:T(128)}, u32[]{:S(2)}) copy-start(f32[8]{0:T(128)} %copy-done.78) | copy-start | bytes 100
  148.3 25.5 %copy-start.52 = (f32[1,512,128]{2,0,1:T(1,128)S(1)}, f32[1,512,128]{2,0,1:T(1,128)}, u32[]{:S(2)}) copy-start(f32[1,512,128]{2,0,1:T(1,128)} %copy.76) | copy-start | bytes 786436
  165.1 15.2 %copy-start.6 = (f32[512,512]{1,0:T(8,128)}, f32[512,512]{1,0:T(8,128)S(1)}, u32[]{:S(2)}) copy-start(f32[512,512]{1,0:T(8,128)S(1)} %tensor_sum.12.base) | copy-start | bytes 3145732
  187.6 17.1 %copy-start.42 = (bf16[128,512]{1,0:T(8,128)(2,1)S(1)}, bf16[128,512]{1,0:T(8,128)(2,1)}, u32[]{:S(2)}) copy-start(bf16[128,512]{1,0:T(8,128)(2,1)} %param.25) | copy-start | bytes 393220
  187.6 17.4 %copy-start.24 = (bf16[1024,512]{1,0:T(8,128)(2,1)S(1)}, bf16[1024,512]{1,0:T(8,128)(2,1)}, u32[]{:S(2)}) copy-start(bf16[1024,512]{1,0:T(8,128)(2,1)} %constant.58.clone) | copy-start | bytes 3145732
  187.6 17.4 %copy-start.50 = (bf16[512,128]{1,0:T(8,128)(2,1)S(1)}, bf16[512,128]{1,0:T(8,128)(2,1)}, u32[]{:S(2)}) copy-start(bf16[512,128]{1,0:T(8,128)(2,1)} %param.23) | copy-start | bytes 393220
  187.7 17.8 %copy-start.10 = (bf16[2,512,512]{2,1,0:T(8,128)(2,1)S(1)}, bf16[2,512,512]{2,1,0:T(8,128)(2,1)}, u32[]{:S(2)}) copy-start(bf16[2,512,512]{2,1,0:T(8,128)(2,1)} %copy-done.9) | copy-start | bytes 3145732
  187.7 17.8 %copy-start.12 = (bf16[512,128]{1,0:T(8,128)(2,1)S(1)}, bf16[512,128]{1,0:T(8,128)(2,1)}, u32[]{:S(2)}) copy-start(bf16[512,128]{1,0:T(8,128)(2,1)} %copy-done.11) | copy-start | bytes 393220
  187.7 17.8 %copy-start.14 = (bf16[512,128]{1,0:T(8,128)(2,1)S(1)}, bf16[512,128]{1,0:T(8,128)(2,1)}, u32[]{:S(2)}) copy-start(bf16[512,128]{1,0:T(8,128)(2,1)} %copy-done.13) | copy-start | bytes 393220
  187.9 21.5 %copy-start.26 = (bf16[512,3,128]{0,2,1:T(8,128)(2,1)S(1)}, bf16[512,3,128]{0,2,1:T(8,128)(2,1)}, u32[]{:S(2)}) copy-start(bf16[512,3,128]{0,2,1:T(8,128)(2,1)} %copy-done.25) | copy-start | bytes 1179652
  187.9 21.5 %copy-start.59 = (f32[1,512]{1,0:T(1,128)S(1)}, f32[1,512]{1,0:T(1,128)}, u32[]{:S(2)}) copy-start(f32[1,512]{1,0:T(1,128)} %copy-done.58) | copy-start | bytes 6148
  187.9 21.5 %copy-start.63 = (f32[512]{0:T(512)S(1)}, f32[512]{0:T(512)}, u32[]{:S(2)}) copy-start(f32[512]{0:T(512)} %copy-done.62) | copy-start | bytes 6148
  210.4 17.1 %copy-start.46 = (bf16[512,512]{1,0:T(8,128)(2,1)S(1)}, bf16[512,512]{1,0:T(8,128)(2,1)}, u32[]{:S(2)}) copy-start(bf16[512,512]{1,0:T(8,128)(2,1)} %param.21) | copy-start | bytes 1572868
  210.4 17.1 %copy-start.94 = (f32[512,512]{1,0:T(8,128)S(1)}, f32[512,512]{1,0:T(8,128)}, u32[]{:S(2)}) copy-start(f32[512,512]{1,0:T(8,128)} %get-tuple-element.129) | copy-start | bytes 3145732
  233.0 17.6 %copy-start.36 = (bf16[1,512,128]{2,1,0:T(8,128)(2,1)S(1)}, bf16[1,512,128]{2,1,0:T(8,128)(2,1)}, u32[]{:S(2)}) copy-start(bf16[1,512,128]{2,1,0:T(8,128)(2,1)} %copy-done.35) | copy-start | bytes 393220
  250.5 118.6 %copy-start.15 = (f32[56,128]{1,0:T(8,128)}, f32[56,128]{1,0:T(8,128)S(1)}, u32[]{:S(2)}) copy-start(f32[56,128]{1,0:T(8,128)S(1)} %exchange_dp.5) | copy-start | bytes 86020
  369.8 16.7 %slice-start.1 = ((f32[56,128]{1,0:T(8,128)}), f32[16,128]{1,0:T(8,128)S(1)}, s32[]{:S(2)}) async-start(f32[56,128]{1,0:T(8,128)} %copy-done.15), calls=%async_computation.2 | async-start | bytes 16384 | tf_op jit(solution)/shard_map/slice | solution.py:239
  370.1 21.8 %slice-start = ((f32[56,128]{1,0:T(8,128)}), f32[4,128]{1,0:T(4,128)S(1)}, s32[]{:S(2)}) async-start(f32[56,128]{1,0:T(8,128)} %copy-done.15), calls=%async_computation.1 | async-start | bytes 4096 | tf_op jit(solution)/shard_map/slice | solution.py:239
  370.2 22.4 %copy-start.16 = (f32[56,128]{1,0:T(8,128)S(1)}, f32[56,128]{1,0:T(8,128)}, u32[]{:S(2)}) copy-start(f32[56,128]{1,0:T(8,128)} %copy-done.15) | copy-start | bytes 86020
  (67 other events, 240.5 us)
Sparse Core Ops, SparseCore 0:
  143.2 102.9 all-reduce.4

commit v3 on v2

--- a/solution.py
+++ b/solution.py
@@ -583,7 +583,6 @@
     result, final_pull = jax.vjp(layer_norm, after_fourth, gain_rows[4])
     grad_four, gain_five = final_pull(output_cotangent.astype(jnp.float32))
     cotangent_in, gain_four, late_in_grad, late_back_grad = fourth_pull(0.5 * grad_four)
-    late_in_grad, late_back_grad = lax.psum((late_in_grad, late_back_grad), "dp")
     grad_three = tensor_sum(grad_four, cotangent_in, 1.0, 4)
     direct_grad, mean_grad, var_grad, scale_grad, shift_grad, second_point_grad = back_pull(
         grad_three
@@ -595,6 +594,16 @@
     cotangent_in, gain_three, first_point_grad, depth_grad = front_pull(mixed_grad)
     grad_two = tensor_sum(grad_three, cotangent_in, 1.0, 5)
     attended_grad, out_grad = out_pull(grad_two)
+    late_in_grad, late_back_grad, second_point_grad, first_point_grad, out_grad = lax.psum(
+        (
+            late_in_grad,
+            late_back_grad,
+            second_point_grad,
+            first_point_grad.reshape(model_width, 2 * local_width),
+            out_grad,
+        ),
+        "dp",
+    )
     qkv_grad, position_grad, bias_grad = attend_back(
         attended_grad.astype(jnp.bfloat16), mixed_qkv, reversed_position, kept, head_count
     )
@@ -602,23 +611,9 @@
     cotangent_in, gain_two, qkv_grad = qkv_pull(qkv_grad.astype(jnp.float32))
     grad_one = tensor_sum(grad_two, cotangent_in, 1.0, 6)
     cotangent_in, gain_one, early_in_grad, early_back_grad = first_pull(0.5 * grad_one)
-    first_point_grad = first_point_grad.reshape(model_width, 2 * local_width)
-    fold = model_width // 2
-    pieces = (
-        early_in_grad,
-        early_back_grad,
-        jnp.concatenate([qkv_grad, pos_grad], axis=1),
-        jnp.concatenate([first_point_grad[:fold], first_point_grad[fold:]], axis=1),
-        out_grad,
-        second_point_grad,
-    )
-    summed = halving_sum(jnp.concatenate(pieces), 12)
-    early_in_grad, early_back_grad, middle_sum, first_sum, out_grad, second_point_grad = jnp.split(
-        summed, np.cumsum([piece.shape[0] for piece in pieces])[:-1].tolist()
-    )
-    first_point_grad = jnp.concatenate(
-        [first_sum[:, : 2 * local_width], first_sum[:, 2 * local_width :]]
-    )
+    pieces = (early_in_grad, early_back_grad, jnp.concatenate([qkv_grad, pos_grad], axis=1))
+    summed = halving_sum(jnp.concatenate(pieces), 12, groups=3)
+    early_in_grad, early_back_grad, middle_sum = jnp.split(summed, 3)
     grad_zero = tensor_sum(grad_one, cotangent_in, 1.0, 7)
     (gain_grads,) = exchange_many(
         (jnp.stack([gain_one, gain_two, gain_three, gain_four]),), "tensor", 10

time: 417 us -> 424 us (1.017)
  Pallas kernels: 283 us -> 291 us
  other arithmetic: 33.6 us -> 27.2 us
    pallas_call x1, Pallas kernels: 114 us -> 122 us  [halving_sum(): pl.pallas_call(functools.partial(halving_kernel, count, groups), out_shap...]
    unnamed x199 -> x244, local copies, waits for them, and re-layouts: 19.8 us -> 28.1 us
  transfers between devices with their start and end apart: 1 -> 1, of which waited for: 0 -> 0; matrix products, arithmetic and copies ran while one was open for 12% -> 6% of each run, Pallas kernels for 50% -> 42%
where the time goes in v3:
time: 424 us; the launch traced here: 417 us
  Pallas kernels  291 us (69%)
  local copies, waits for them, and re-layouts  41.6 us (10%)
  matrix products  41 us (10%)
  other arithmetic  27.2 us (6%)
  between operations  16 us (4%)
    pallas_call x8, Pallas kernels, tensor_sum(): pl.pallas_call(functools.partial(tensor_kernel, factor, chunks), out_shap...  134 us
    pallas_call x1, Pallas kernels, halving_sum(): pl.pallas_call(functools.partial(halving_kernel, count, groups), out_shap...  122 us
    unnamed x244, local copies, waits for them, and re-layouts  28.1 us
    pallas_call x4, Pallas kernels, exchange_sum(): pl.pallas_call(functools.partial(exchange_kernel, axis, count), out_shape...  27.9 us
    dot_general x24, matrix products, matmul(): jnp.dot(first_factor, second_factor, preferred_element_type=jnp.float32)  25 us
    conv_general_dilated x3, matrix products, depthwise_conv(): lax.conv_general_dilated(gated, kernel[:, None, :], (1,), [(half, half)],...  11 us
  transfers between devices with their start and end apart: 1, of which 0 were waited for; matrix products, arithmetic and copies ran while one was open for 6% of the time, Pallas kernels for 42%

profile of v3, /device:TPU:0, one launch (start us, length us, event | category | flops | bytes accessed | tf_op | source)
XLA Modules:
  0.0 416.7 jit_solution(11951215849600215563)
XLA Ops:
  15.6 17.7 %tensor_sum.8.base = f32[512,512]{1,0:T(8,128)S(1)} custom-call(f32[512,512]{1,0:T(8,128)S(1)} %fusion.48.part, f32[512,512]{1,0:T(8,128)S(1)} %convert_element_type.49.base), custom_call_target="tpu_custom_call" | custom-call | tf_op jit(solution)/shard_map/tensor_sum/pallas_call | solution.py:141
  36.4 3.0 attend.1
  42.8 16.8 %tensor_sum.9.base = f32[512,512]{1,0:T(8,128)S(1)} custom-call(f32[512,512]{1,0:T(8,128)S(1)} %fusion.50.part, f32[512,512]{1,0:T(8,128)S(1)} %tensor_sum.8.base), custom_call_target="tpu_custom_call" | custom-call | tf_op jit(solution)/shard_map/tensor_sum/pallas_call | solution.py:141
  66.5 1.8 copy.74
  68.3 2.9 fusion.41
  72.0 7.6 %exchange_dp.3 = f32[8,128]{1,0:T(8,128)S(1)} custom-call(f32[8,128]{1,0:T(8,128)S(1)} %maximum_maximum_fusion.1.part), custom_call_target="tpu_custom_call" | custom-call | tf_op jit(solution)/shard_map/exchange_dp/pallas_call | solution.py:203
  81.2 16.1 %tensor_sum.10.base = f32[512,512]{1,0:T(8,128)S(1)} custom-call(f32[512,512]{1,0:T(8,128)S(1)} %fusion.23.part, f32[512,512]{1,0:T(8,128)S(1)} %tensor_sum.9.base), custom_call_target="tpu_custom_call" | custom-call | tf_op jit(solution)/shard_map/tensor_sum/pallas_call | solution.py:141
  98.3 2.0 reduce_sum.293
  107.2 16.8 %tensor_sum.11 = f32[512,512]{1,0:T(8,128)S(1)} custom-call(f32[512,512]{1,0:T(8,128)S(1)} %fusion.51.part, f32[512,512]{1,0:T(8,128)S(1)} %copy-done.3), custom_call_target="tpu_custom_call" | custom-call | tf_op jit(solution)/shard_map/tensor_sum/pallas_call | solution.py:141
  125.0 2.0 reduce_sum.295
  127.7 1.9 fusion.2
  129.6 2.5 fusion.3
  132.1 1.9 multiply_convert_fusion.1
  138.0 16.8 %tensor_sum.12.base = f32[512,512]{1,0:T(8,128)S(1)} custom-call(f32[512,512]{1,0:T(8,128)S(1)} %broadcast_add_fusion.3.part, f32[512,512]{1,0:T(8,128)S(1)} %get-tuple-element.108.base), custom_call_target="tpu_custom_call" | custom-call | tf_op jit(solution)/shard_map/tensor_sum/pallas_call | solution.py:141
  156.8 6.7 %exchange_dp.4 = f32[8,128]{1,0:T(8,128)S(1)} custom-call(f32[8,128]{1,0:T(8,128)S(1)} %maximum_maximum_fusion.2.part), custom_call_target="tpu_custom_call" | custom-call | tf_op jit(solution)/shard_map/exchange_dp/pallas_call | solution.py:203
  164.4 2.2 fusion.25
  166.6 1.8 copy.80
  169.8 2.2 multiply_reduce_fusion.1
  178.3 16.0 %tensor_sum.13.base = f32[512,512]{1,0:T(8,128)S(1)} custom-call(f32[512,512]{1,0:T(8,128)S(1)} %broadcast_add_fusion.2.part, f32[512,512]{1,0:T(8,128)S(1)} %copy-done.9), custom_call_target="tpu_custom_call" | custom-call | tf_op jit(solution)/shard_map/tensor_sum/pallas_call | solution.py:141
  196.3 2.2 copy.93
  201.6 3.8 attend_back.1
  207.3 16.7 %tensor_sum.14.base = f32[512,512]{1,0:T(8,128)S(1)} custom-call(f32[512,512]{1,0:T(8,128)S(1)} %broadcast_add_fusion.1.part, f32[512,512]{1,0:T(8,128)S(1)} %copy-done.11), custom_call_target="tpu_custom_call" | custom-call | tf_op jit(solution)/shard_map/tensor_sum/pallas_call | solution.py:141
  227.2 4.0 exchange_tensor.1
  231.3 5.9 %fusion.47 = f32[31,1,128]{2,1,0:T(1,128)S(1)} fusion(f32[1,512,128]{2,0,1:T(1,128)S(1)} %copy-done.65, f32[1,512,128]{2,0,1:T(1,128)S(1)} %bitcast.149), kind=kOutput, calls=%fused_computation.141 | convolution fusion | flops 24010752 | bytes 540160 | tf_op jit(solution)/shard_map/transpose(jvp())/conv_general_dilated | solution.py:490
  237.5 9.6 %exchange_dp.5 = f32[56,128]{1,0:T(8,128)S(1)} custom-call(f32[56,128]{1,0:T(8,128)S(1)} %concatenate.20.part), custom_call_target="tpu_custom_call" | custom-call | tf_op jit(solution)/shard_map/exchange_dp/pallas_call | solution.py:203
  247.1 1.7 fusion.55
  250.9 1.7 fusion.52
  253.0 122.1 %halving_sum.1 = f32[1536,512]{1,0:T(8,128)S(1)} custom-call(f32[1536,512]{1,0:T(8,128)S(1)} %maximum_maximum_fusion.part), custom_call_target="tpu_custom_call" | custom-call | tf_op jit(solution)/shard_map/halving_sum/pallas_call | solution.py:454
  378.5 17.2 %tensor_sum.15 = f32[512,512]{1,0:T(8,128)S(1)} custom-call(f32[512,512]{1,0:T(8,128)S(1)} %broadcast_add_fusion.part, f32[512,512]{1,0:T(8,128)S(1)} %tensor_sum.14.base), custom_call_target="tpu_custom_call" | custom-call | tf_op jit(solution)/shard_map/tensor_sum/pallas_call | solution.py:141
  398.9 3.0 fusion.45
  403.0 1.9 copy.126
  404.9 1.9 copy.127
  (348 shorter events, 70.5 us)
Async XLA Ops:
  7.2 97.3 %copy-start = (bf16[512,512]{1,0:T(8,128)(2,1)S(1)}, bf16[512,512]{1,0:T(8,128)(2,1)}, u32[]{:S(2)}) copy-start(bf16[512,512]{1,0:T(8,128)(2,1)} %param.31) | copy-start | bytes 1572868
  7.2 394.7 %all-reduce.5.cloned.1.call-start = ((), (), s32[]{:S(2)}) async-start(), calls=%async_computation | async-start | bytes 6291456 | tf_op jit(solution)/shard_map/psum | solution.py:597
  12.2 21.6 %copy-start.75 = (f32[1,512]{1,0:T(1,128)}, f32[1,512]{1,0:T(1,128)S(1)}, u32[]{:S(2)}) copy-start(f32[1,512]{1,0:T(1,128)S(1)} %get-tuple-element.119) | copy-start | bytes 6148
  15.5 18.4 %copy-start.64 = (bf16[512,3,128]{2,0,1:T(8,128)(2,1)S(1)}, bf16[512,3,128]{2,0,1:T(8,128)(2,1)}, u32[]{:S(2)}) copy-start(bf16[512,3,128]{2,0,1:T(8,128)(2,1)} %param.22) | copy-start | bytes 1179652
  15.5 18.6 %copy-start.107 = (bf16[2,2,64]{2,1,0:T(2,128)(2,1)S(1)}, bf16[2,2,64]{2,1,0:T(2,128)(2,1)}, u32[]{:S(2)}) copy-start(bf16[2,2,64]{2,1,0:T(2,128)(2,1)} %param.24) | copy-start | bytes 1540
  34.0 7.7 %copy-start.30 = (bf16[512,512]{1,0:T(8,128)(2,1)}, bf16[512,512]{1,0:T(8,128)(2,1)S(1)}, u32[]{:S(2)}) copy-start(bf16[512,512]{1,0:T(8,128)(2,1)S(1)} %multiply_convert_fusion.6) | copy-start | bytes 1572868
  34.2 7.5 %copy-start.35 = (bf16[512,3,128]{0,2,1:T(8,128)(2,1)}, bf16[512,3,128]{0,2,1:T(8,128)(2,1)S(1)}, u32[]{:S(2)}) copy-start(bf16[512,3,128]{0,2,1:T(8,128)(2,1)S(1)} %copy.72) | copy-start | bytes 1179652
  61.0 10.2 %copy-start.71 = (f32[512]{0:T(512)}, f32[512]{0:T(512)S(1)}, u32[]{:S(2)}) copy-start(f32[512]{0:T(512)S(1)} %broadcast_multiply_fusion.2) | copy-start | bytes 6148
  68.3 11.3 %copy-start.113 = (bf16[128]{0:T(256)(128)(2,1)S(1)}, bf16[128]{0:T(256)(128)(2,1)}, u32[]{:S(2)}) copy-start(bf16[128]{0:T(256)(128)(2,1)} %param.29) | copy-start | bytes 772
  68.3 11.3 %copy-start.114 = (bf16[128]{0:T(256)(128)(2,1)S(1)}, bf16[128]{0:T(256)(128)(2,1)}, u32[]{:S(2)}) copy-start(bf16[128]{0:T(256)(128)(2,1)} %param.28) | copy-start | bytes 772
  68.3 12.7 %copy-start.69 = (bf16[128,512]{1,0:T(8,128)(2,1)S(1)}, bf16[128,512]{1,0:T(8,128)(2,1)}, u32[]{:S(2)}) copy-start(bf16[128,512]{1,0:T(8,128)(2,1)} %param.30) | copy-start | bytes 393220
  71.2 8.4 %copy-start.55 = (f32[1,512,128]{2,0,1:T(1,128)}, f32[1,512,128]{2,0,1:T(1,128)S(1)}, u32[]{:S(2)}) copy-start(f32[1,512,128]{2,0,1:T(1,128)S(1)} %get-tuple-element.127) | copy-start | bytes 786436
  127.7 7.1 %copy-start.116 = (f32[512,512]{1,0:T(8,128)S(1)}, f32[512,512]{1,0:T(8,128)}, u32[]{:S(2)}) copy-start(f32[512,512]{1,0:T(8,128)} %get-tuple-element.129) | copy-start | bytes 3145732
  137.8 18.1 %copy-start.56 = (f32[1,512,128]{2,0,1:T(1,128)S(1)}, f32[1,512,128]{2,0,1:T(1,128)}, u32[]{:S(2)}) copy-start(f32[1,512,128]{2,0,1:T(1,128)} %copy-done.55) | copy-start | bytes 786436
  137.8 18.0 %copy-start.70 = (bf16[128,512]{1,0:T(8,128)(2,1)S(1)}, bf16[128,512]{1,0:T(8,128)(2,1)}, u32[]{:S(2)}) copy-start(bf16[128,512]{1,0:T(8,128)(2,1)} %param.30) | copy-start | bytes 393220
  137.8 18.0 %copy-start.102 = (f32[128]{0:T(128)S(1)}, f32[128]{0:T(128)}, u32[]{:S(2)}) copy-start(f32[128]{0:T(128)} %copy-done.101) | copy-start | bytes 1540
  137.8 18.0 %copy-start.104 = (f32[128]{0:T(128)S(1)}, f32[128]{0:T(128)}, u32[]{:S(2)}) copy-start(f32[128]{0:T(128)} %copy-done.103) | copy-start | bytes 1540
  137.8 18.0 %copy-start.106 = (f32[128]{0:T(128)S(1)}, f32[128]{0:T(128)}, u32[]{:S(2)}) copy-start(f32[128]{0:T(128)} %copy-done.105) | copy-start | bytes 1540
  137.8 18.0 %copy-start.111 = (f32[128]{0:T(128)S(1)}, f32[128]{0:T(128)}, u32[]{:S(2)}) copy-start(f32[128]{0:T(128)} %copy-done.110) | copy-start | bytes 1540
  138.0 18.8 %copy-start.100 = (f32[8]{0:T(128)S(1)}, f32[8]{0:T(128)}, u32[]{:S(2)}) copy-start(f32[8]{0:T(128)} %copy-done.99) | copy-start | bytes 100
  154.8 9.6 %copy-start.112 = (bf16[31,128]{1,0:T(8,128)(2,1)S(1)}, bf16[31,128]{1,0:T(8,128)(2,1)}, u32[]{:S(2)}) copy-start(bf16[31,128]{1,0:T(8,128)(2,1)} %param.27) | copy-start | bytes 23812
  206.5 17.6 %copy-start.60 = (bf16[512,512]{1,0:T(8,128)(2,1)S(1)}, bf16[512,512]{1,0:T(8,128)(2,1)}, u32[]{:S(2)}) copy-start(bf16[512,512]{1,0:T(8,128)(2,1)} %param.21) | copy-start | bytes 1572868
  206.6 17.6 %copy-start.115 = (f32[512,512]{1,0:T(8,128)S(1)}, f32[512,512]{1,0:T(8,128)}, u32[]{:S(2)}) copy-start(f32[512,512]{1,0:T(8,128)} %get-tuple-element.126) | copy-start | bytes 3145732
  231.3 15.8 %copy-start.17 = (bf16[1024,128]{1,0:T(8,128)(2,1)S(1)}, bf16[1024,128]{1,0:T(8,128)(2,1)}, u32[]{:S(2)}) copy-start(bf16[1024,128]{1,0:T(8,128)(2,1)} %copy-done.16) | copy-start | bytes 786436
  231.3 17.5 %copy-start.13 = (bf16[512,384]{1,0:T(8,128)(2,1)S(1)}, bf16[512,384]{1,0:T(8,128)(2,1)}, u32[]{:S(2)}) copy-start(bf16[512,384]{1,0:T(8,128)(2,1)} %copy-done.12) | copy-start | bytes 1179652
  231.3 17.5 %copy-start.31 = (bf16[512,512]{1,0:T(8,128)(2,1)S(1)}, bf16[512,512]{1,0:T(8,128)(2,1)}, u32[]{:S(2)}) copy-start(bf16[512,512]{1,0:T(8,128)(2,1)} %copy-done.30) | copy-start | bytes 1572868
  247.0 130.4 %copy-start.22 = (f32[56,128]{1,0:T(8,128)}, f32[56,128]{1,0:T(8,128)S(1)}, u32[]{:S(2)}) copy-start(f32[56,128]{1,0:T(8,128)S(1)} %exchange_dp.5) | copy-start | bytes 86020
  253.0 125.1 %copy-start.27 = (f32[512,512]{1,0:T(8,128)S(1)}, f32[512,512]{1,0:T(8,128)}, u32[]{:S(2)}) copy-start(f32[512,512]{1,0:T(8,128)} %copy-done.26) | copy-start | bytes 3145732
  378.1 17.6 %slice-start.1 = ((f32[56,128]{1,0:T(8,128)}), f32[16,128]{1,0:T(8,128)S(1)}, s32[]{:S(2)}) async-start(f32[56,128]{1,0:T(8,128)} %copy-done.22), calls=%async_computation.2 | async-start | bytes 16384 | tf_op jit(solution)/shard_map/slice | solution.py:239
  378.5 19.3 %slice-start = ((f32[56,128]{1,0:T(8,128)}), f32[4,128]{1,0:T(4,128)S(1)}, s32[]{:S(2)}) async-start(f32[56,128]{1,0:T(8,128)} %copy-done.22), calls=%async_computation.1 | async-start | bytes 4096 | tf_op jit(solution)/shard_map/slice | solution.py:239
  378.5 20.0 %copy-start.23 = (f32[56,128]{1,0:T(8,128)S(1)}, f32[56,128]{1,0:T(8,128)}, u32[]{:S(2)}) copy-start(f32[56,128]{1,0:T(8,128)} %copy-done.22) | copy-start | bytes 86020
  402.0 7.4 %copy-start.1 = (bf16[512,512]{1,0:T(8,128)(2,1)S(1)}, bf16[512,512]{1,0:T(8,128)(2,1)}, u32[]{:S(2)}) copy-start(bf16[512,512]{1,0:T(8,128)(2,1)} %param.31) | copy-start | bytes 1572868
  (88 other events, 250.4 us)
Sparse Core Ops, SparseCore 0:
  198.6 166.5 all-reduce.4
